TPU v7x, 512 devices: a whole 4x8x8 slice. The times are simulated.
512 devices in a mesh: depth: 8 (over z), block: 64 (over x, y, core).
Axes of the slice: x: 4, y: 8, z: 8, core: 2. Of those that a mesh axis runs over, the one named last changes fastest.
Arguments:
- sensitivity: float32 [16384, 8, 1024], P(('depth', 'block')), as said below
- owners: int32 [16384, 8], P(('depth', 'block')), may hold values from 0 to 63, all different within a row; in each aligned block of 32 rows (0 to 31, 32 to 63, ...) at most 8 rows name the same one
- local_block: int32 [16384, 8], P(('depth', 'block')), may hold values from 0 to 3
- station_ids: int32 [16384], P(('depth', 'block')), may hold values from 0 to 1023
- kept: int32 [16384], P(('depth', 'block')), may hold values 0 or 1
- times: float32 [16384], P(('depth', 'block')), may hold values from -6 to 6
- hit_counts: int32 [8, 256, 128], P('depth', 'block'), may hold values from 0 to 63
Outputs:
- model_update: float32 [8, 256, 128], P('depth', 'block')
- station_update: float32 [1024], replicated
- ray_direction: float32 [16384], P(('depth', 'block'))
Inputs may be any that keep to these rules, and one draw needn't show every extreme that they name: Within a row the 8 owners differ; in the rows of one device no owner is named more than 8 times, and in some device one owner exactly 8 times. `sensitivity`: every entry is at most 16 / sqrt(8192) in magnitude.
All inputs are finite; a program needn't handle non-finite values. No bound on the sum of `kept` on one device may be relied on, other than what follows from the above.
Results may differ from a plain program's by a relative error of at most 0.0003.
Values sent between devices are 32-bit elements; how exact they have to be, the bound alone decides.
A program may use at most 64 MiB of HBM per device.

v0:
```python
import jax
import jax.numpy as jnp
from jax import lax
from jax.sharding import PartitionSpec as P

NSTA = 1024
ITERS = 2


epsilon = 1e-06


def per_device(sensitivity, owners, local_block, station_ids, kept, times, hit_counts):
    ray_dev, slots, width = sensitivity.shape
    lay_dev, blk_dev, cells = hit_counts.shape
    highest = lax.Precision.HIGHEST
    column_scale = 1.0 / jnp.sqrt(1.0 + hit_counts.astype(jnp.float32))
    kept_rows = kept.astype(jnp.float32)
    station_onehot = (station_ids[:, None] == jnp.arange(NSTA, dtype=jnp.int32)[None, :]).astype(
        jnp.float32
    )
    n_block = lax.axis_size("block")
    capacity = 2 * ray_dev * slots // n_block
    buffer_rows = n_block * capacity
    flat_owner = owners.reshape(-1)
    owner_onehot = (flat_owner[:, None] == jnp.arange(n_block, dtype=jnp.int32)[None, :]).astype(
        jnp.int32
    )
    ranks = jnp.sum((jnp.cumsum(owner_onehot, axis=0) - 1) * owner_onehot, axis=1)
    places = flat_owner * capacity + ranks
    send_rows = (
        jnp.zeros((buffer_rows, width), jnp.float32).at[places].set(sensitivity.reshape(-1, width))
    )
    send_index = (
        jnp.full((buffer_rows,), -1.0, jnp.float32)
        .at[places]
        .set(local_block.reshape(-1).astype(jnp.float32))
    )
    got_rows, got_index = (
        lax.all_to_all(
            send_rows.reshape(n_block, capacity, width),
            "block",
            split_axis=0,
            concat_axis=0,
            tiled=True,
        ),
        lax.all_to_all(
            send_index.reshape(n_block, capacity), "block", split_axis=0, concat_axis=0, tiled=True
        ),
    )
    got_rows = got_rows.reshape(buffer_rows, width)
    got_index = got_index.reshape(buffer_rows)
    selector = (got_index[:, None] == jnp.arange(blk_dev).astype(jnp.float32)[None, :]).astype(
        jnp.float32
    )

    def kernel_adjoint(weights):
        per_slot = jnp.broadcast_to(weights[:, None], (ray_dev, slots)).reshape(-1)
        send_weights = jnp.zeros((buffer_rows,), jnp.float32).at[places].set(per_slot)
        received = lax.all_to_all(
            send_weights.reshape(n_block, capacity),
            "block",
            split_axis=0,
            concat_axis=0,
            tiled=True,
        ).reshape(-1)
        grad = jnp.dot((selector * received[:, None]).T, got_rows, precision=highest)
        layers = width // cells
        grad = grad.reshape(blk_dev, layers, cells).transpose(1, 0, 2)
        return lax.psum_scatter(grad, "depth", scatter_dimension=0, tiled=True)

    def station_part(weights):
        return jnp.dot(weights, station_onehot, precision=highest)

    def normalize(raw):
        local_squares = jnp.sum(raw * raw)
        total = lax.psum(local_squares, ("depth", "block"))
        beta_value = jnp.sqrt(total + epsilon)
        unit = raw / beta_value
        stations = lax.psum(station_part(unit), ("depth", "block"))
        model = kernel_adjoint(unit) * column_scale
        return (beta_value, unit, model, stations)

    def model_norm(model, stations):
        total = lax.psum(jnp.sum(model * model), ("depth", "block"))
        return jnp.sqrt(total + jnp.sum(stations * stations) + epsilon)

    beta_value, unit, grad_model, grad_station = normalize(kept_rows * times)
    alpha_value = model_norm(grad_model, grad_station)
    dir_model = grad_model / alpha_value
    dir_station = grad_station / alpha_value
    search_model, search_station = (dir_model, dir_station)
    sol_model = jnp.zeros_like(dir_model)
    sol_station = jnp.zeros_like(dir_station)
    phi_bar = beta_value
    rho_bar = alpha_value
    for iteration in range(ITERS):
        gathered = lax.all_gather(dir_model * column_scale, "depth", axis=0, tiled=True)
        kernel_layers = gathered.shape[0]
        columns = gathered.transpose(0, 2, 1).reshape(kernel_layers * cells, blk_dev)
        product = jnp.dot(got_rows, columns, precision=highest)
        values = jnp.sum(product * selector, axis=1)
        returned = lax.all_to_all(
            values.reshape(n_block, capacity), "block", split_axis=0, concat_axis=0, tiled=True
        )
        kernel = jnp.sum(returned.reshape(-1)[places].reshape(ray_dev, slots), axis=1)
        raw = (
            kept_rows * (kernel + jnp.dot(station_onehot, dir_station, precision=highest))
            - alpha_value * unit
        )
        beta_value, unit, grad_model, grad_station = normalize(raw)
        grad_model = grad_model - beta_value * dir_model
        grad_station = grad_station - beta_value * dir_station
        alpha_value = model_norm(grad_model, grad_station)
        dir_model = grad_model / alpha_value
        dir_station = grad_station / alpha_value
        rho_value = jnp.sqrt(rho_bar * rho_bar + beta_value * beta_value)
        cosine = rho_bar / rho_value
        sine_value = beta_value / rho_value
        theta_value = sine_value * alpha_value
        rho_bar = -cosine * alpha_value
        phi_value = cosine * phi_bar
        phi_bar = sine_value * phi_bar
        sol_model = sol_model + phi_value / rho_value * search_model
        sol_station = sol_station + phi_value / rho_value * search_station
        search_model = dir_model - theta_value / rho_value * search_model
        search_station = dir_station - theta_value / rho_value * search_station
    return (column_scale * sol_model, sol_station, unit)


def solution(mesh):
    in_specs = (
        P(("depth", "block"), None, None),
        P(("depth", "block"), None),
        P(("depth", "block"), None),
        P(("depth", "block")),
        P(("depth", "block")),
        P(("depth", "block")),
        P("depth", "block", None),
    )
    out_specs = (P("depth", "block", None), P(), P(("depth", "block")))
    return jax.shard_map(
        per_device, mesh=mesh, in_specs=in_specs, out_specs=out_specs, check_vma=False
    )
```

profile of v0, /device:TPU:1, one launch (start us, length us, event | category | flops | bytes accessed | tf_op | source)
XLA Modules:
  0.0 761.9 jit_solution(889671313559040942)
XLA Ops:
  0.6 0.9 copy.17
  1.7 0.7 broadcast_multiply_fusion
  3.3 1.3 multiply_reduce_fusion.6
  4.7 106.1 %psum.49 = f32[]{:T(128)} all-reduce(f32[]{:T(128)} %multiply_reduce_fusion.6), channel_id=1, replica_groups=mesh['depth'=8,'block'=64] {'depth','block'}, use_global_device_ids=true, to_apply=%region_5.6 | all-reduce | flops 1 | bytes 8 | tf_op jit(solution)/shard_map/psum | solution.py:77
  112.5 1.4 scatter_custom_fusion.1
  114.5 6.7 all-to-all-start.1
  122.1 1.4 scatter_custom_fusion
  124.2 6.3 all-to-all-done.1
  130.6 4.6 all-to-all-start
  135.2 2.9 scatter_custom_fusion.2
  138.1 6.5 all-to-all-done
  144.6 4.9 all-to-all-start.2
  149.5 1.3 dynamic-slice
  151.6 0.7 reduce.17
  152.4 0.7 reduce.18
  153.2 47.7 %all-to-all-done.2 = f32[64,8,1024]{2,1,0:T(8,128)S(1)} async-done(((f32[64,8,1024]{2,1,0:T(8,128)}), f32[64,8,1024]{2,1,0:T(8,128)S(1)}, u32[]{:S(2)}, u32[]{:S(2)}) %all-to-all-start.2) | async-done | bytes 2097184 | tf_op jit(solution)/shard_map/all_to_all | solution.py:40
  200.9 1.9 copy.23
  202.8 3.4 convolution_bitcast_fusion.1
  206.2 22.4 %all-reduce = f32[8,4,128]{2,1,0:T(4,128)S(1)} all-reduce(f32[8,4,128]{2,1,0:T(4,128)S(1)} %convolution_bitcast_fusion.1), channel_id=2, replica_groups=mesh['depth'=8,'block'=64] {'depth'}, use_global_device_ids=true, to_apply=%region_8.9.clone | all-reduce | flops 4096 | bytes 32768
  228.5 1.2 multiply_reduce_fusion.3
  229.7 101.0 %all-reduce.3 = (f32[]{:T(128)}, f32[1024]{0:T(1024)S(1)}) all-reduce(f32[]{:T(128)} %multiply_reduce_fusion.3, f32[1024]{0:T(1024)S(1)} %bitcast.105), channel_id=1, replica_groups=mesh['depth'=8,'block'=64] {'depth','block'}, use_global_device_ids=true, to_apply=%region_10.11 | all-reduce | flops 1025 | bytes 8200 | tf_op jit(solution)/shard_map/psum | solution.py:85
  333.3 15.6 %all_gather.6 = f32[8,4,128]{2,1,0:T(4,128)S(1)} all-gather(f32[1,4,128]{2,1,0:T(4,128)S(1)} %fusion.60), channel_id=1, replica_groups=mesh['depth'=8,'block'=64] {'depth'}, dimensions={0}, use_global_device_ids=true | all-gather | bytes 18432 | tf_op jit(solution)/shard_map/all_gather | solution.py:98
  348.9 1.9 fusion.10
  350.8 0.7 all_to_all.38
  351.5 11.9 %all-to-all-start.3 = ((f32[64,1,8]{2,1,0:T(1,128)}), f32[64,1,8]{2,1,0:T(1,128)S(1)}, u32[]{:S(2)}, u32[]{:S(2)}) async-start(f32[64,1,8]{2,1,0:T(1,128)} %bitcast.16), calls=%async_computation.3 | async-start | bytes 65536 | tf_op jit(solution)/shard_map/all_to_all | solution.py:103
  363.4 9.3 %all-to-all-done.3 = f32[64,1,8]{2,1,0:T(1,128)S(1)} async-done(((f32[64,1,8]{2,1,0:T(1,128)}), f32[64,1,8]{2,1,0:T(1,128)S(1)}, u32[]{:S(2)}, u32[]{:S(2)}) %all-to-all-start.3) | async-done | bytes 2080 | tf_op jit(solution)/shard_map/all_to_all | solution.py:103
  372.7 0.7 reduce.19
  373.5 1.9 gather_fusion
  375.7 0.8 multiply_reduce_fusion.5
  376.5 94.4 %psum.52 = f32[]{:T(128)} all-reduce(f32[]{:T(128)} %get-tuple-element.7), channel_id=1, replica_groups=mesh['depth'=8,'block'=64] {'depth','block'}, use_global_device_ids=true, to_apply=%region_16.17 | all-reduce | flops 1 | bytes 8 | tf_op jit(solution)/shard_map/psum | solution.py:77
  471.8 1.4 scatter_custom_fusion.3
  473.9 7.1 all-to-all-start.4
  481.5 8.9 %all-to-all-done.4 = f32[64,1,8]{2,1,0:T(1,128)S(1)} async-done(((f32[64,1,8]{2,1,0:T(1,128)}), f32[64,1,8]{2,1,0:T(1,128)S(1)}, u32[]{:S(2)}, u32[]{:S(2)}) %all-to-all-start.4) | async-done | bytes 2080 | tf_op jit(solution)/shard_map/all_to_all | solution.py:60
  490.3 0.7 reduce.20
  491.2 3.4 convolution_bitcast_fusion
  494.5 21.3 %all-reduce.1 = f32[8,4,128]{2,1,0:T(4,128)S(1)} all-reduce(f32[8,4,128]{2,1,0:T(4,128)S(1)} %convolution_bitcast_fusion), channel_id=3, replica_groups=mesh['depth'=8,'block'=64] {'depth'}, use_global_device_ids=true, to_apply=%region_18.19.clone | all-reduce | flops 4096 | bytes 32768
  515.9 1.2 multiply_reduce_fusion.2
  517.1 99.5 %all-reduce.2 = (f32[]{:T(128)}, f32[1024]{0:T(1024)S(1)}) all-reduce(f32[]{:T(128)} %multiply_reduce_fusion.2, f32[1024]{0:T(1024)S(1)} %bitcast.104), channel_id=1, replica_groups=mesh['depth'=8,'block'=64] {'depth','block'}, use_global_device_ids=true, to_apply=%region_20.21 | all-reduce | flops 1025 | bytes 8200 | tf_op jit(solution)/shard_map/psum | solution.py:85
  619.2 15.5 %all_gather.7 = f32[8,4,128]{2,1,0:T(4,128)S(1)} all-gather(f32[1,4,128]{2,1,0:T(4,128)S(1)} %fusion.49), channel_id=1, replica_groups=mesh['depth'=8,'block'=64] {'depth'}, dimensions={0}, use_global_device_ids=true | all-gather | bytes 18432 | tf_op jit(solution)/shard_map/all_gather | solution.py:98
  634.6 1.9 fusion.13
  636.5 0.7 all_to_all.42
  637.2 14.1 %all-to-all-start.5 = ((f32[64,1,8]{2,1,0:T(1,128)}), f32[64,1,8]{2,1,0:T(1,128)S(1)}, u32[]{:S(2)}, u32[]{:S(2)}) async-start(f32[64,1,8]{2,1,0:T(1,128)} %bitcast.26), calls=%async_computation.5 | async-start | bytes 65536 | tf_op jit(solution)/shard_map/all_to_all | solution.py:103
  651.4 9.2 %all-to-all-done.5 = f32[64,1,8]{2,1,0:T(1,128)S(1)} async-done(((f32[64,1,8]{2,1,0:T(1,128)}), f32[64,1,8]{2,1,0:T(1,128)S(1)}, u32[]{:S(2)}, u32[]{:S(2)}) %all-to-all-start.5) | async-done | bytes 2080 | tf_op jit(solution)/shard_map/all_to_all | solution.py:103
  660.6 0.7 reduce.21
  661.4 1.9 gather_fusion.1
  663.6 0.9 multiply_reduce_fusion.4
  664.4 94.3 %psum.55 = f32[]{:T(128)} all-reduce(f32[]{:T(128)} %get-tuple-element.9), channel_id=1, replica_groups=mesh['depth'=8,'block'=64] {'depth','block'}, use_global_device_ids=true, to_apply=%region_26.27 | all-reduce | flops 1 | bytes 8 | tf_op jit(solution)/shard_map/psum | solution.py:77
  760.2 1.2 add_multiply_fusion
  (53 shorter events, 10.6 us)
Async XLA Ops:
  0.6 134.6 %copy-start = (f32[32,8,1024]{2,1,0:T(8,128)S(1)}, f32[32,8,1024]{2,1,0:T(8,128)}, u32[]{:S(2)}) copy-start(f32[32,8,1024]{2,1,0:T(8,128)} %param.7) | copy-start | bytes 3145732
  114.5 16.0 %all-to-all-start.1 = ((f32[64,1,8]{2,1,0:T(1,128)}), f32[64,1,8]{2,1,0:T(1,128)S(1)}, u32[]{:S(2)}, u32[]{:S(2)}) async-start(f32[64,1,8]{2,1,0:T(1,128)} %bitcast.4), calls=%async_computation.1 | async-start | bytes 65536 | tf_op jit(solution)/shard_map/all_to_all | solution.py:60
  130.6 14.0 %all-to-all-start = ((f32[64,1,8]{2,1,0:T(1,128)}), f32[64,1,8]{2,1,0:T(1,128)S(1)}, u32[]{:S(2)}, u32[]{:S(2)}) async-start(f32[64,1,8]{2,1,0:T(1,128)} %bitcast.3), calls=%async_computation | async-start | bytes 65536 | tf_op jit(solution)/shard_map/all_to_all | solution.py:47
  144.6 6.2 copy-start.3
  144.6 56.3 %all-to-all-start.2 = ((f32[64,8,1024]{2,1,0:T(8,128)}), f32[64,8,1024]{2,1,0:T(8,128)S(1)}, u32[]{:S(2)}, u32[]{:S(2)}) async-start(f32[64,8,1024]{2,1,0:T(8,128)} %bitcast.96), calls=%async_computation.2 | async-start | bytes 4194304 | tf_op jit(solution)/shard_map/all_to_all | solution.py:40
  202.7 25.8 %copy-start.1 = (s32[1,4,128]{2,1,0:T(4,128)S(1)}, s32[1,4,128]{2,1,0:T(4,128)}, u32[]{:S(2)}) copy-start(s32[1,4,128]{2,1,0:T(4,128)} %param.13) | copy-start | bytes 6148
  206.2 169.5 %copy-start.2 = (s32[32]{0:T(128)S(1)}, s32[32]{0:T(128)}, u32[]{:S(2)}) copy-start(s32[32]{0:T(128)} %param.11) | copy-start | bytes 388
  351.5 21.2 %all-to-all-start.3 = ((f32[64,1,8]{2,1,0:T(1,128)}), f32[64,1,8]{2,1,0:T(1,128)S(1)}, u32[]{:S(2)}, u32[]{:S(2)}) async-start(f32[64,1,8]{2,1,0:T(1,128)} %bitcast.16), calls=%async_computation.3 | async-start | bytes 65536 | tf_op jit(solution)/shard_map/all_to_all | solution.py:103
  473.9 16.4 %all-to-all-start.4 = ((f32[64,1,8]{2,1,0:T(1,128)}), f32[64,1,8]{2,1,0:T(1,128)S(1)}, u32[]{:S(2)}, u32[]{:S(2)}) async-start(f32[64,1,8]{2,1,0:T(1,128)} %bitcast.19), calls=%async_computation.4 | async-start | bytes 65536 | tf_op jit(solution)/shard_map/all_to_all | solution.py:60
  637.2 23.3 %all-to-all-start.5 = ((f32[64,1,8]{2,1,0:T(1,128)}), f32[64,1,8]{2,1,0:T(1,128)S(1)}, u32[]{:S(2)}, u32[]{:S(2)}) async-start(f32[64,1,8]{2,1,0:T(1,128)} %bitcast.26), calls=%async_computation.5 | async-start | bytes 65536 | tf_op jit(solution)/shard_map/all_to_all | solution.py:103
where the time goes:
time: 763 us; the launch traced here: 762 us
  blocking collectives  570 us (75%)
  waiting for transfers between devices  87.8 us (12%)
  starting transfers between devices  49.3 us (6%)
  local copies, waits for them, and re-layouts  20.6 us (3%)
  other arithmetic  15.3 us (2%)
  matrix products  12.7 us (2%)
    psum x3, blocking collectives, normalize(): total = lax.psum(local_squares, ('depth', 'block'))  295 us
    psum x2, blocking collectives, model_norm(): total = lax.psum(jnp.sum(model * model), ('depth', 'block'))  200 us
    all_to_all x1, waiting for transfers between devices, per_device(): lax.all_to_all(send_rows.reshape(n_block, capacity, width), 'block', spli...  47.7 us
    unnamed x2, blocking collectives  43.7 us
    all_gather x2, blocking collectives, per_device(): lax.all_gather(dir_model * column_scale, 'depth', axis=0, tiled=True)  31.1 us
    all_to_all x2, starting transfers between devices, per_device(): lax.all_to_all(values.reshape(n_block, capacity), 'block', split_axis=0,...  25.9 us
    all_to_all x2, waiting for transfers between devices, per_device(): lax.all_to_all(values.reshape(n_block, capacity), 'block', split_axis=0,...  18.5 us
  transfers between devices with their start and end apart: 6, of which 6 were waited for; matrix products, arithmetic and copies ran while one was open for 1% of the time, Pallas kernels for 0%

commit v1 on v0

v1 whole, which is shorter than its diff:
```python
import functools

import jax
import jax.numpy as jnp
from jax import lax
from jax.experimental import pallas as pl
from jax.experimental.pallas import tpu as pltpu
from jax.sharding import PartitionSpec as P

NX, NY, NZ = 4, 8, 8
EPS = 1e-06
F32 = jnp.float32
BF16 = jnp.bfloat16
HIGHEST = lax.Precision.HIGHEST
MESH = pl.DeviceIdType.MESH

META, ROWS, CSZ, CSY, CST, FX, FY, FZ = range(8)
S1X, S1Y, S1Z, S2Y, S2Z, S2X, S3Z, S3Y, A2Y, A2Z, A2X, A1X, A1Y, A1Z, EX = range(15)
STAGES = 8 + 2 * 15


def iota(shape, dim):
    return lax.broadcasted_iota(jnp.int32, shape, dim)


def total(tile):
    return jnp.sum(jnp.sum(tile, axis=0, keepdims=True), axis=1, keepdims=True)


def split(value):
    high = value.astype(BF16)
    return high, (value - high.astype(F32)).astype(BF16)


def dot(a, b):
    return jnp.dot(a, b, preferred_element_type=F32)


def dot_nt(a, b):
    return lax.dot_general(
        a, b, (((1,), (1,)), ((), ())), precision=HIGHEST, preferred_element_type=F32
    )


def kernel(
    sens, owners, local_block, station_ids, kept, times, hits,
    out_model, out_station, out_ray,
    rows, meta, ohr, ohc, cs_own, csz, csy, cst, fin, fx, fy, fz,
    sx, sy, sz, rx, ry, rz, s2y, s2z, s2x, r2y, r2z, r2x, s3z, s3y, r3z, r3y,
    a2y, a2z, a2x, g2y, g2z, g2x, a1x, gx, gy, gz, ex,
    local_sem, send_sem, recv_sem,
):
    z = lax.axis_index("depth")
    b = lax.axis_index("block")
    c = lax.rem(b, 2)
    y = lax.rem(lax.div(b, 2), NY)
    x = lax.div(b, 2 * NY)
    axes = {
        "x": (NX, x, lambda p: (z, (p * NY + y) * 2 + c)),
        "y": (NY, y, lambda p: (z, (x * NY + p) * 2 + c)),
        "z": (NZ, z, lambda p: (p, b)),
    }
    sibling = (z, (x * NY + y) * 2 + 1 - c)

    own_rows = pltpu.make_async_copy(
        sens.at[:, :, pl.ds(pl.multiple_of(c * 512, 512), 512)], rows.at[c], local_sem
    )
    own_rows.start()

    barrier = pltpu.get_barrier_semaphore()
    pl.semaphore_signal(barrier, inc=1, device_id=sibling, device_id_type=MESH)
    for name in "xyz":
        n, me, peer = axes[name]
        for step in range(1, n):
            pl.semaphore_signal(
                barrier, inc=1, device_id=peer(lax.rem(me + step, n)), device_id_type=MESH
            )

    blocks = (owners[...] * 4 + local_block[...]).astype(F32)
    eye8 = (iota((8, 8), 0) == iota((8, 8), 1)).astype(F32)
    spread = (lax.shift_right_logical(iota((32, 256), 1), 3) == iota((32, 256), 0)).astype(F32)
    by_slot = jnp.dot(
        dot_nt(eye8, blocks), spread, precision=HIGHEST, preferred_element_type=F32
    )
    slot_of = jnp.bitwise_and(iota((8, 256), 1), 7)
    block_row = jnp.sum(
        jnp.where(iota((8, 256), 0) == slot_of, by_slot, 0.0), axis=0, keepdims=True
    )
    keep = kept[...].astype(F32)
    ids = station_ids[...]
    scale = 1.0 / jnp.sqrt(1.0 + hits[0].astype(F32))
    meta[c] = jnp.zeros((2, 8, 128), F32)
    meta[c, 0, 0:1, :] = block_row[:, 0:128]
    meta[c, 0, 1:2, :] = block_row[:, 128:256]
    meta[c, 0, 2:3, 0:32] = keep * times[...]
    meta[c, 0, 3:4, 0:32] = keep
    meta[c, 0, 4:5, 0:32] = lax.shift_right_logical(ids, 7).astype(F32)
    meta[c, 0, 5:6, 0:32] = jnp.bitwise_and(ids, 127).astype(F32)
    meta[c, 1, 0:4, :] = jnp.where(c == 0, scale, 0.0)
    meta[c, 1, 4:8, :] = jnp.where(c == 1, scale, 0.0)

    pl.semaphore_wait(barrier, 1 + (NX - 1) + (NY - 1) + (NZ - 1))

    pending = []

    def send(stage, src, dst, device):
        copy = pltpu.make_async_remote_copy(
            src_ref=src, dst_ref=dst, send_sem=send_sem.at[stage], recv_sem=recv_sem.at[stage],
            device_id=device, device_id_type=MESH,
        )
        copy.start()
        return copy

    def spread_out(stage, name, source, buffer):
        n, me, peer = axes[name]
        for step in range(1, n):
            p = lax.rem(me + step, n)
            send(stage, source(p), buffer.at[me], peer(p))
        others = buffer.at[pl.ds(0, n - 1)]
        pending.append((stage, others))

    def arrived(stage, name, buffer):
        n = axes[name][0]
        others = buffer.at[pl.ds(0, n - 1)]
        pltpu.make_async_remote_copy(
            src_ref=others, dst_ref=others, send_sem=send_sem.at[stage],
            recv_sem=recv_sem.at[stage], device_id=sibling, device_id_type=MESH,
        ).wait_recv()

    meta_copy = send(META, meta.at[c], meta.at[c], sibling)
    rows_copy = send(
        ROWS, sens.at[:, :, pl.ds(pl.multiple_of((1 - c) * 512, 512), 512)], rows.at[c], sibling
    )
    meta_copy.wait_recv()

    cs_own[...] = meta[0, 1] + meta[1, 1]
    csz[z] = cs_own[...]
    csy[y] = cs_own[...]
    spread_out(CSY, "y", lambda p: cs_own, csy)
    spread_out(CSZ, "z", lambda p: cs_own, csz)

    raw = [meta[k, 0, 2:3, 0:32] for k in range(2)]
    keeps = [meta[k, 0, 3:4, 0:32] for k in range(2)]
    station_high = [
        meta[k, 0, 4:5, 0:32] == iota((8, 32), 0).astype(F32) for k in range(2)
    ]
    station_low = [
        (meta[k, 0, 5:6, 0:32] == iota((128, 32), 0).astype(F32)).astype(F32) for k in range(2)
    ]
    ray_of = lax.shift_right_logical(iota((256, 32), 0), 3) == iota((256, 32), 1)
    sub = iota((256, 128), 0)
    lane = iota((256, 128), 1)
    for k in range(2):
        column = jnp.zeros((256, 1), F32)
        for h in range(2):
            part = meta[k, 0, h : h + 1, :]
            ohr[k, :, 128 * h : 128 * h + 128] = (
                jnp.where(part == sub.astype(F32), 1.0, 0.0).astype(BF16)
            )
            column += jnp.sum(
                jnp.where(sub == lane + 128 * h, part, 0.0), axis=1, keepdims=True
            )
        for h in range(2):
            ohc[k, :, 128 * h : 128 * h + 128] = (
                jnp.where(column == (lane + 128 * h).astype(F32), 1.0, 0.0).astype(BF16)
            )

    own_rows.wait()
    rows_copy.wait_recv()

    def adjoint_and_reduce(it, ray):
        stage = 8 + 15 * it
        square = ray[0] * ray[0] + ray[1] * ray[1]
        stations = jnp.zeros((8, 128), F32)
        for k in range(2):
            stations += dot_nt(jnp.where(station_high[k], ray[k], 0.0), station_low[k])
        columns = [
            jnp.sum(jnp.where(ray_of, ray[k], 0.0), axis=1, keepdims=True) for k in range(2)
        ]
        for p in range(NX):
            sx[it, p, 16] = stations
            sx[it, p, 17] = jnp.zeros((8, 128), F32)
            sx[it, p, 17, 0:1, 0:32] = square

        def grad(half):
            result = None
            for k in range(2):
                part = rows[k, :, :, 256 * half : 256 * half + 256].reshape(256, 256)
                for piece in split(part * columns[k]):
                    term = dot(ohr[k], piece)
                    result = term if result is None else result + term
            return result

        value = grad(0)
        for p in range(NX):
            for j in range(2):
                sx[it, p, 8 * j : 8 * j + 8] = value[
                    64 * p : 64 * p + 64, 128 * j : 128 * j + 128
                ].reshape(8, 8, 128)
        spread_out(stage + S1X, "x", lambda p: sx.at[it, p], rx.at[it])
        value = grad(1)
        value_y = value[:, 0:128].reshape(NX, NY, 8, 128)
        value_z = value[:, 128:256].reshape(NX, NZ, 8, 128)
        for p in range(NY):
            sy[it, p] = value_y[:, p]
        spread_out(stage + S1Y, "y", lambda p: sy.at[it, p], ry.at[it])
        for p in range(NZ):
            sz[it, p] = value_z[:, p]
        spread_out(stage + S1Z, "z", lambda p: sz.at[it, p], rz.at[it])
        rx[it, x] = sx[it, x]
        ry[it, y] = sy[it, y]
        rz[it, z] = sz[it, z]

        def summed(buffer, n):
            result = buffer[it, 0]
            for p in range(1, n):
                result = result + buffer[it, p]
            return result

        if it == 0:
            arrived(CSY, "y", csy)
            cst[z] = csy[z]
            spread_out(CST, "z", lambda p: csy.at[p], cst)

        arrived(stage + S1X, "x", rx.at[it])
        sum_x = summed(rx, NX)
        for p in range(NY):
            s2y[it, p, 0] = sum_x[p]
            s2y[it, p, 1] = sum_x[16]
            s2y[it, p, 2] = sum_x[17]
        spread_out(stage + S2Y, "y", lambda p: s2y.at[it, p], r2y.at[it])
        for p in range(NZ):
            s2z[it, p, 0] = sum_x[8 + p]
        spread_out(stage + S2Z, "z", lambda p: s2z.at[it, p], r2z.at[it])
        r2y[it, y] = s2y[it, y]
        r2z[it, z] = s2z[it, z]

        arrived(stage + S1Y, "y", ry.at[it])
        sum_y = summed(ry, NY)
        for p in range(NX):
            s2x[it, p, 0] = sum_y[p]
        arrived(stage + S1Z, "z", rz.at[it])
        sum_z = summed(rz, NZ)
        for p in range(NX):
            s2x[it, p, 1] = sum_z[p]
        spread_out(stage + S2X, "x", lambda p: s2x.at[it, p], r2x.at[it])
        r2x[it, x] = s2x[it, x]

        arrived(stage + S2Y, "y", r2y.at[it])
        from_y = summed(r2y, NY)
        s3z[it, 0] = from_y[0]
        s3z[it, 2] = from_y[1]
        s3z[it, 3] = from_y[2]
        arrived(stage + S2Z, "z", r2z.at[it])
        s3y[it, 0] = summed(r2z, NZ)[0]
        arrived(stage + S2X, "x", r2x.at[it])
        from_x = summed(r2x, NX)
        s3z[it, 1] = from_x[0]
        s3y[it, 1] = from_x[1]
        spread_out(stage + S3Z, "z", lambda p: s3z.at[it], r3z.at[it])
        spread_out(stage + S3Y, "y", lambda p: s3y.at[it], r3y.at[it])
        r3z[it, z] = s3z[it]
        r3y[it, y] = s3y[it]
        arrived(stage + S3Z, "z", r3z.at[it])
        from_z = summed(r3z, NZ)
        arrived(stage + S3Y, "y", r3y.at[it])
        from_y = summed(r3y, NY)
        tiles = [from_z[0], from_y[0], from_z[1], from_y[1]]
        return tiles, from_z[2], jnp.sqrt(total(from_z[3]) + EPS)

    def gather(it, grads, scales):
        stage = 8 + 15 * it
        a2y[it, 0] = scales[0] * grads[0]
        a2y[it, 1] = grads[0] * grads[0] + grads[2] * grads[2]
        a2z[it, 0] = scales[1] * grads[1]
        a2z[it, 1] = grads[1] * grads[1] + grads[3] * grads[3]
        a2x[it, 0] = scales[2] * grads[2]
        a2x[it, 1] = scales[3] * grads[3]
        spread_out(stage + A2Y, "y", lambda p: a2y.at[it], g2y.at[it])
        spread_out(stage + A2Z, "z", lambda p: a2z.at[it], g2z.at[it])
        spread_out(stage + A2X, "x", lambda p: a2x.at[it], g2x.at[it])
        g2y[it, y] = a2y[it]
        g2z[it, z] = a2z[it]
        g2x[it, x] = a2x[it]
        arrived(stage + A2Y, "y", g2y.at[it])
        arrived(stage + A2Z, "z", g2z.at[it])
        square = None
        for p in range(NY):
            a1x[it, p] = g2y[it, p, 0]
            a1x[it, 8 + p] = g2z[it, p, 0]
            term = g2y[it, p, 1] + g2z[it, p, 1]
            square = term if square is None else square + term
        a1x[it, 16] = square
        spread_out(stage + A1X, "x", lambda p: a1x.at[it], gx.at[it])
        arrived(stage + A2X, "x", g2x.at[it])
        for p in range(NX):
            gy[it, y, p] = g2x[it, p, 0]
            gz[it, z, p] = g2x[it, p, 1]
        spread_out(stage + A1Y, "y", lambda p: gy.at[it, y], gy.at[it])
        spread_out(stage + A1Z, "z", lambda p: gz.at[it, z], gz.at[it])
        gx[it, x] = a1x[it]
        arrived(stage + A1X, "x", gx.at[it])
        square = gx[it, 0, 16]
        for p in range(1, NX):
            square = square + gx[it, p, 16]
        return square

    def forward(it, square):
        stage = 8 + 15 * it
        sums = [None, None]

        def add(half, values):
            pieces = split(values)
            for k in range(2):
                picked = dot(ohc[k], pieces[0]) + dot(ohc[k], pieces[1])
                part = rows[k, :, :, 256 * half : 256 * half + 256].reshape(256, 256) * picked
                part = part[:, 0:128] + part[:, 128:256]
                sums[k] = part if sums[k] is None else sums[k] + part

        add(
            0,
            jnp.concatenate(
                [gx[it, :, 0:8].reshape(256, 128), gx[it, :, 8:16].reshape(256, 128)], axis=1
            ),
        )
        arrived(stage + A1Y, "y", gy.at[it])
        arrived(stage + A1Z, "z", gz.at[it])
        add(
            1,
            jnp.concatenate(
                [
                    jnp.concatenate(
                        [buffer[it, :, p].reshape(64, 128) for p in range(NX)], axis=0
                    )
                    for buffer in (gy, gz)
                ],
                axis=1,
            ),
        )
        ex[it, c] = jnp.zeros((4, 8, 128), F32)
        for k in range(2):
            column = jnp.sum(sums[k], axis=1, keepdims=True)
            ex[it, c, 0, k : k + 1, 0:32] = jnp.sum(
                jnp.where(ray_of, column, 0.0), axis=0, keepdims=True
            )
        ex[it, c, 1] = square
        if it == 1:
            layer = lax.rem(z, 4)
            for i in range(2):
                ex[it, c, 2 + i] = jnp.where(
                    layer == 0,
                    gx[i, x, y],
                    jnp.where(
                        layer == 1, gx[i, x, 8 + y], jnp.where(layer == 2, gy[i, y, x], gz[i, y, x])
                    ),
                )
        copy = send(stage + EX, ex.at[it, c], ex.at[it, c], sibling)
        pending.append((stage + EX, ex.at[it, c]))
        copy.wait_recv()
        values = ex[it, 0, 0] + ex[it, 1, 0]
        return [values[k : k + 1, 0:32] for k in range(2)], total(ex[it, 0, 1] + ex[it, 1, 1])

    def station_values(stations):
        return [
            jnp.sum(
                jnp.where(
                    station_high[k],
                    jnp.dot(
                        stations, station_low[k], precision=HIGHEST, preferred_element_type=F32
                    ),
                    0.0,
                ),
                axis=0,
                keepdims=True,
            )
            for k in range(2)
        ]

    sums, station_sum, beta0 = adjoint_and_reduce(0, raw)
    unit = [raw[k] / beta0 for k in range(2)]
    arrived(CSZ, "z", csz)
    arrived(CST, "z", cst)
    first = 4 * c
    scales = [csz[first], cst[first + 1], csz[first + 2], cst[first + 3]]
    grads0 = [scales[j] * sums[j] / beta0 for j in range(4)]
    grad_station0 = station_sum / beta0
    square = gather(0, grads0, scales)
    product, model_square = forward(0, square)
    alpha0 = jnp.sqrt(model_square + total(grad_station0 * grad_station0) + EPS)
    dir_station0 = grad_station0 / alpha0

    at_station = station_values(dir_station0)
    raw = [
        keeps[k] * (product[k] / alpha0 + at_station[k]) - alpha0 * unit[k] for k in range(2)
    ]
    sums, station_sum, beta1 = adjoint_and_reduce(1, raw)
    unit = [raw[k] / beta1 for k in range(2)]
    grads1 = [scales[j] * sums[j] / beta1 - beta1 * (grads0[j] / alpha0) for j in range(4)]
    grad_station1 = station_sum / beta1 - beta1 * dir_station0
    square = gather(1, grads1, scales)
    product, model_square = forward(1, square)
    alpha1 = jnp.sqrt(model_square + total(grad_station1 * grad_station1) + EPS)
    dir_station1 = grad_station1 / alpha1
    rho = jnp.sqrt(alpha0 * alpha0 + beta1 * beta1)
    cosine = alpha0 / rho
    sine = beta1 / rho
    theta = sine * alpha1
    rho_bar = -cosine * alpha1
    step0 = cosine * beta0 / rho
    phi_bar = sine * beta0
    turn = theta / rho

    at_station = station_values(dir_station1)
    raw = [
        keeps[k] * (product[k] / alpha1 + at_station[k]) - alpha1 * unit[k] for k in range(2)
    ]
    fin[...] = jnp.zeros((3, 8, 128), F32)
    fin[0, 0:1, 0:32] = raw[0] * raw[0] + raw[1] * raw[1]
    spread_out(FX, "x", lambda p: fin.at[0], fx)
    fx[x] = fin[0]
    arrived(FX, "x", fx)
    fin[1] = jnp.sum(fx[...], axis=0)
    spread_out(FY, "y", lambda p: fin.at[1], fy)
    fy[y] = fin[1]
    arrived(FY, "y", fy)
    fin[2] = jnp.sum(fy[...], axis=0)
    spread_out(FZ, "z", lambda p: fin.at[2], fz)
    fz[z] = fin[2]
    arrived(FZ, "z", fz)
    beta2 = jnp.sqrt(total(jnp.sum(fz[...], axis=0)) + EPS)
    rho = jnp.sqrt(rho_bar * rho_bar + beta2 * beta2)
    step1 = rho_bar / rho * phi_bar / rho

    weight0 = (step0 - step1 * turn) / alpha0
    weight1 = step1 / alpha1
    holder = lax.div(z, 4)
    model = weight0 * ex[1, holder, 2] + weight1 * ex[1, holder, 3]
    out_model[0] = jnp.where(c == 0, model[0:4], model[4:8])
    out_station[...] = (step0 - step1 * turn) * dir_station0 + step1 * dir_station1
    out_ray[...] = jnp.where(c == 0, raw[0], raw[1]) / beta2

    meta_copy.wait_send()
    rows_copy.wait_send()
    for stage, others in pending:
        pltpu.make_async_remote_copy(
            src_ref=others, dst_ref=others, send_sem=send_sem.at[stage],
            recv_sem=recv_sem.at[stage], device_id=sibling, device_id_type=MESH,
        ).wait_send()


def per_device(sensitivity, owners, local_block, station_ids, kept, times, hit_counts):
    vmem = pl.BlockSpec(memory_space=pltpu.VMEM)

    def tiles(*shape):
        return pltpu.VMEM(shape + (8, 128), F32)

    model, station, ray = pl.pallas_call(
        kernel,
        out_shape=(
            jax.ShapeDtypeStruct((1, 4, 128), F32),
            jax.ShapeDtypeStruct((8, 128), F32),
            jax.ShapeDtypeStruct((1, 32), F32),
        ),
        in_specs=[pl.BlockSpec(memory_space=pl.ANY)] + [vmem] * 6,
        out_specs=(vmem,) * 3,
        scratch_shapes=[
            pltpu.VMEM((2, 32, 8, 512), F32),
            tiles(2, 2),
            pltpu.VMEM((2, 256, 256), BF16),
            pltpu.VMEM((2, 256, 256), BF16),
            tiles(), tiles(NZ), tiles(NY), tiles(NZ),
            tiles(3), tiles(NX), tiles(NY), tiles(NZ),
            tiles(2, NX, 18), tiles(2, NY, 4), tiles(2, NZ, 4),
            tiles(2, NX, 18), tiles(2, NY, 4), tiles(2, NZ, 4),
            tiles(2, NY, 3), tiles(2, NZ, 1), tiles(2, NX, 2),
            tiles(2, NY, 3), tiles(2, NZ, 1), tiles(2, NX, 2),
            tiles(2, 4), tiles(2, 2), tiles(2, NZ, 4), tiles(2, NY, 2),
            tiles(2, 2), tiles(2, 2), tiles(2, 2),
            tiles(2, NY, 2), tiles(2, NZ, 2), tiles(2, NX, 2),
            tiles(2, 17), tiles(2, NX, 17), tiles(2, NY, 4), tiles(2, NZ, 4),
            tiles(2, 2, 4),
            pltpu.SemaphoreType.DMA,
            pltpu.SemaphoreType.DMA((STAGES,)),
            pltpu.SemaphoreType.DMA((STAGES,)),
        ],
        compiler_params=pltpu.CompilerParams(
            collective_id=0, has_side_effects=True, vmem_limit_bytes=40 * 1024 * 1024
        ),
    )(
        sensitivity, owners, local_block, station_ids.reshape(1, 32), kept.reshape(1, 32),
        times.reshape(1, 32), hit_counts,
    )
    return model, station.reshape(1024), ray.reshape(32)


def solution(mesh):
    in_specs = (
        P(("depth", "block"), None, None),
        P(("depth", "block"), None),
        P(("depth", "block"), None),
        P(("depth", "block")),
        P(("depth", "block")),
        P(("depth", "block")),
        P("depth", "block", None),
    )
    out_specs = (P("depth", "block", None), P(), P(("depth", "block")))
    return jax.shard_map(
        per_device, mesh=mesh, in_specs=in_specs, out_specs=out_specs, check_vma=False
    )
```

time: 763 us -> 95.9 us (0.13)
  blocking collectives: 570 us -> 0 us
  Pallas kernels: 0 us -> 90 us
  waiting for transfers between devices: 87.8 us -> 0 us
  starting transfers between devices: 49.3 us -> 0 us
  local copies, waits for them, and re-layouts: 20.6 us -> 4.97 us
  other arithmetic: 15.3 us -> 0 us
  matrix products: 12.7 us -> 0 us
    psum x5 -> x0, blocking collectives: 495 us -> none  [the longest x3 295 us: normalize(): total = lax.psum(local_squares, ('depth', 'block'))]
    pallas_call x0 -> x1, Pallas kernels: none -> 90 us  [per_device(): pl.pallas_call(kernel, out_shape=(jax.ShapeDtypeStruct((1, 4, 128), F32),...]
    all_to_all x6 -> x0, waiting for transfers between devices: 87.8 us -> none  [the longest x1 47.7 us: per_device(): lax.all_to_all(send_rows.reshape(n_block, capacity, width), 'block', spli...]
    all_to_all x6 -> x0, starting transfers between devices: 49.3 us -> none  [the longest x2 25.9 us: per_device(): lax.all_to_all(values.reshape(n_block, capacity), 'block', split_axis=0,...]
    unnamed x2 -> x0, blocking collectives: 43.7 us -> none
    all_gather x2 -> x0, blocking collectives: 31.1 us -> none  [per_device(): lax.all_gather(dir_model * column_scale, 'depth', axis=0, tiled=True)]
    dot_general x8 -> x0, matrix products: 12.7 us -> none  [the longest x2 6.79 us: kernel_adjoint(): jnp.dot((selector * received[:, None]).T, got_rows, precision=highest)]
  transfers between devices with their start and end apart: 6 -> 0, of which waited for: 6 -> 0; matrix products, arithmetic and copies ran while one was open for 1% -> 0% of each run, Pallas kernels for 0% -> 0%
where the time goes in v1:
time: 95.9 us; the launch traced here: 95.6 us
  Pallas kernels  90 us (94%)
  local copies, waits for them, and re-layouts  4.97 us (5%)
    pallas_call x1, Pallas kernels, per_device(): pl.pallas_call(kernel, out_shape=(jax.ShapeDtypeStruct((1, 4, 128), F32),...  90 us
    unnamed x19, local copies, waits for them, and re-layouts  4.97 us

profile of v1, /device:TPU:1, one launch (start us, length us, event | category | flops | bytes accessed | tf_op | source)
XLA Modules:
  0.0 95.6 jit_solution(1075779225188090988)
XLA Ops:
  0.6 0.0 copy-start.5
  0.6 0.7 copy-done.5
  1.3 0.0 copy-start.6
  1.3 0.1 copy.10.owners
  1.4 0.6 copy-done.6
  2.0 0.0 copy-start.1
  2.0 0.0 copy-start.2
  2.0 0.0 copy-start.3
  2.0 0.0 copy-start.4
  2.0 0.1 copy.11.local_block
  2.1 0.6 copy-done.1
  2.7 0.0 copy-done.2
  2.7 0.0 copy-done.3
  2.7 0.0 copy-done.4
  2.7 0.0 copy-start
  2.7 1.2 %copy-done = f32[32,8,1024]{2,1,0:T(8,128)S(1)} copy-done((f32[32,8,1024]{2,1,0:T(8,128)S(1)}, f32[32,8,1024]{2,1,0:T(8,128)}, u32[]{:S(2)}) %copy-start) | copy-done | bytes 1048600
  3.9 90.0 %shard_map.94 = (f32[1,4,128]{2,1,0:T(4,128)S(1)}, f32[8,128]{1,0:T(8,128)S(1)}, f32[1,32]{1,0:T(1,128)S(1)}) custom-call(f32[32,8,1024]{2,1,0:T(8,128)S(1)} %copy-done, s32[32,8]{1,0:T(8,128)S(1)} %copy.10.owners, s32[32,8]{1,0:T(8,128)S(1)} %copy.11.local_block, s32[1,32]{1,0:T(1,128)S(1)} %bitcast.6, s32[1,32]{1,0:T(1,128)S(1)} %bitcast.7, ...), custom_call_target="tpu_custom_call" | custom-call | tf_op jit(solution)/shard_map/pallas_call | solution.py:457
  93.9 0.6 copy.15
  94.5 0.6 copy.16
  95.1 0.5 copy.17
Async XLA Ops:
  0.6 0.7 copy-start.5
  1.3 0.7 copy-start.6
  2.0 0.7 copy-start.1
  2.0 0.7 copy-start.2
  2.0 0.7 copy-start.3
  2.0 0.7 copy-start.4
  2.7 1.2 %copy-start = (f32[32,8,1024]{2,1,0:T(8,128)S(1)}, f32[32,8,1024]{2,1,0:T(8,128)}, u32[]{:S(2)}) copy-start(f32[32,8,1024]{2,1,0:T(8,128)} %sens.1) | copy-start | bytes 3145732

commit v2 on v1

--- a/solution.py
+++ b/solution.py
@@ -14,7 +14,7 @@
 HIGHEST = lax.Precision.HIGHEST
 MESH = pl.DeviceIdType.MESH
 
-META, ROWS, CSZ, CSY, CST, FX, FY, FZ = range(8)
+META, ROWS, CSZ, CSY, CST, FW, FZ, UNUSED = range(8)
 S1X, S1Y, S1Z, S2Y, S2Z, S2X, S3Z, S3Y, A2Y, A2Z, A2X, A1X, A1Y, A1Z, EX = range(15)
 STAGES = 8 + 2 * 15
 
@@ -43,12 +43,12 @@
 
 
 def kernel(
-    sens, owners, local_block, station_ids, kept, times, hits,
+    sens, owners_in, local_in, station_in, kept_in, times_in, hits_in,
     out_model, out_station, out_ray,
-    rows, meta, ohr, ohc, cs_own, csz, csy, cst, fin, fx, fy, fz,
+    rows, meta, ohr, ohc, cs_own, csz, csy, cst, fin, fw, fz,
     sx, sy, sz, rx, ry, rz, s2y, s2z, s2x, r2y, r2z, r2x, s3z, s3y, r3z, r3y,
     a2y, a2z, a2x, g2y, g2z, g2x, a1x, gx, gy, gz, ex,
-    local_sem, send_sem, recv_sem,
+    owners, local_block, station_ids, kept, times, hits, local_sem, send_sem, recv_sem,
 ):
     z = lax.axis_index("depth")
     b = lax.axis_index("block")
@@ -59,29 +59,44 @@
         "x": (NX, x, lambda p: (z, (p * NY + y) * 2 + c)),
         "y": (NY, y, lambda p: (z, (x * NY + p) * 2 + c)),
         "z": (NZ, z, lambda p: (p, b)),
+        "xy": (NX * NY, x * NY + y, lambda p: (z, p * 2 + c)),
     }
     sibling = (z, (x * NY + y) * 2 + 1 - c)
 
     own_rows = pltpu.make_async_copy(
-        sens.at[:, :, pl.ds(pl.multiple_of(c * 512, 512), 512)], rows.at[c], local_sem
-    )
+        sens.at[:, :, pl.ds(pl.multiple_of(c * 512, 512), 512)], rows.at[c], local_sem.at[6]
+    )
+    fetches = [
+        pltpu.make_async_copy(src, dst, local_sem.at[i])
+        for i, (src, dst) in enumerate(
+            (
+                (owners_in, owners),
+                (local_in, local_block),
+                (station_in, station_ids),
+                (kept_in, kept),
+                (times_in, times),
+                (hits_in, hits),
+            )
+        )
+    ]
+    for fetch in fetches:
+        fetch.start()
     own_rows.start()
 
     barrier = pltpu.get_barrier_semaphore()
     pl.semaphore_signal(barrier, inc=1, device_id=sibling, device_id_type=MESH)
-    for name in "xyz":
+    for name in ("z", "xy"):
         n, me, peer = axes[name]
         for step in range(1, n):
             pl.semaphore_signal(
                 barrier, inc=1, device_id=peer(lax.rem(me + step, n)), device_id_type=MESH
             )
+    for fetch in fetches:
+        fetch.wait()
 
     blocks = (owners[...] * 4 + local_block[...]).astype(F32)
-    eye8 = (iota((8, 8), 0) == iota((8, 8), 1)).astype(F32)
     spread = (lax.shift_right_logical(iota((32, 256), 1), 3) == iota((32, 256), 0)).astype(F32)
-    by_slot = jnp.dot(
-        dot_nt(eye8, blocks), spread, precision=HIGHEST, preferred_element_type=F32
-    )
+    by_slot = jnp.dot(blocks, spread, precision=HIGHEST, preferred_element_type=F32)
     slot_of = jnp.bitwise_and(iota((8, 256), 1), 7)
     block_row = jnp.sum(
         jnp.where(iota((8, 256), 0) == slot_of, by_slot, 0.0), axis=0, keepdims=True
@@ -99,7 +114,27 @@
     meta[c, 1, 0:4, :] = jnp.where(c == 0, scale, 0.0)
     meta[c, 1, 4:8, :] = jnp.where(c == 1, scale, 0.0)
 
-    pl.semaphore_wait(barrier, 1 + (NX - 1) + (NY - 1) + (NZ - 1))
+    eye32 = iota((32, 32), 0) == iota((32, 32), 1)
+    sub = iota((256, 128), 0)
+    lane = iota((256, 128), 1)
+
+    def one_hots(k, parts):
+        column = jnp.zeros((256, 1), F32)
+        for h in range(2):
+            ohr[k, :, 128 * h : 128 * h + 128] = (
+                jnp.where(parts[h] == sub.astype(F32), 1.0, 0.0).astype(BF16)
+            )
+            column += jnp.sum(
+                jnp.where(sub == lane + 128 * h, parts[h], 0.0), axis=1, keepdims=True
+            )
+        for h in range(2):
+            ohc[k, :, 128 * h : 128 * h + 128] = (
+                jnp.where(column == (lane + 128 * h).astype(F32), 1.0, 0.0).astype(BF16)
+            )
+
+    one_hots(c, [block_row[:, 0:128], block_row[:, 128:256]])
+
+    pl.semaphore_wait(barrier, 1 + (NX * NY - 1) + (NZ - 1))
 
     pending = []
 
@@ -111,13 +146,23 @@
         copy.start()
         return copy
 
-    def spread_out(stage, name, source, buffer):
-        n, me, peer = axes[name]
-        for step in range(1, n):
-            p = lax.rem(me + step, n)
+    def spread_out(*parts):
+        sends = []
+        for stage, name, source, buffer in parts:
+            n, me, peer = axes[name]
+            for step in range(1, n):
+                away = min(step, n - step)
+                if name == "xy":
+                    away = min(step // NY, NX - step // NY) + min(step % NY, NY - step % NY)
+                sends.append((-away, len(sends), stage, name, source, buffer, step))
+            pending.append((stage, buffer.at[pl.ds(0, n - 1)]))
+        for away, order, stage, name, source, buffer, step in sorted(sends, key=lambda t: t[:2]):
+            n, me, peer = axes[name]
+            if name == "xy":
+                p = lax.rem(x + step // NY, NX) * NY + lax.rem(y + step % NY, NY)
+            else:
+                p = lax.rem(me + step, n)
             send(stage, source(p), buffer.at[me], peer(p))
-        others = buffer.at[pl.ds(0, n - 1)]
-        pending.append((stage, others))
 
     def arrived(stage, name, buffer):
         n = axes[name][0]
@@ -136,8 +181,7 @@
     cs_own[...] = meta[0, 1] + meta[1, 1]
     csz[z] = cs_own[...]
     csy[y] = cs_own[...]
-    spread_out(CSY, "y", lambda p: cs_own, csy)
-    spread_out(CSZ, "z", lambda p: cs_own, csz)
+    spread_out((CSY, "y", lambda p: cs_own, csy), (CSZ, "z", lambda p: cs_own, csz))
 
     raw = [meta[k, 0, 2:3, 0:32] for k in range(2)]
     keeps = [meta[k, 0, 3:4, 0:32] for k in range(2)]
@@ -147,23 +191,7 @@
     station_low = [
         (meta[k, 0, 5:6, 0:32] == iota((128, 32), 0).astype(F32)).astype(F32) for k in range(2)
     ]
-    ray_of = lax.shift_right_logical(iota((256, 32), 0), 3) == iota((256, 32), 1)
-    sub = iota((256, 128), 0)
-    lane = iota((256, 128), 1)
-    for k in range(2):
-        column = jnp.zeros((256, 1), F32)
-        for h in range(2):
-            part = meta[k, 0, h : h + 1, :]
-            ohr[k, :, 128 * h : 128 * h + 128] = (
-                jnp.where(part == sub.astype(F32), 1.0, 0.0).astype(BF16)
-            )
-            column += jnp.sum(
-                jnp.where(sub == lane + 128 * h, part, 0.0), axis=1, keepdims=True
-            )
-        for h in range(2):
-            ohc[k, :, 128 * h : 128 * h + 128] = (
-                jnp.where(column == (lane + 128 * h).astype(F32), 1.0, 0.0).astype(BF16)
-            )
+    one_hots(1 - c, [meta[1 - c, 0, h : h + 1, :] for h in range(2)])
 
     own_rows.wait()
     rows_copy.wait_recv()
@@ -174,9 +202,12 @@
         stations = jnp.zeros((8, 128), F32)
         for k in range(2):
             stations += dot_nt(jnp.where(station_high[k], ray[k], 0.0), station_low[k])
-        columns = [
-            jnp.sum(jnp.where(ray_of, ray[k], 0.0), axis=1, keepdims=True) for k in range(2)
-        ]
+        columns = []
+        for k in range(2):
+            column = jnp.sum(jnp.where(eye32, ray[k], 0.0), axis=1, keepdims=True)
+            column = jnp.broadcast_to(column, (32, 128)).reshape(32, 1, 128)
+            column = jnp.broadcast_to(column, (32, 8, 128)).reshape(256, 128)
+            columns.append(jnp.concatenate([column, column], axis=1))
         for p in range(NX):
             sx[it, p, 16] = stations
             sx[it, p, 17] = jnp.zeros((8, 128), F32)
@@ -197,16 +228,17 @@
                 sx[it, p, 8 * j : 8 * j + 8] = value[
                     64 * p : 64 * p + 64, 128 * j : 128 * j + 128
                 ].reshape(8, 8, 128)
-        spread_out(stage + S1X, "x", lambda p: sx.at[it, p], rx.at[it])
+        spread_out((stage + S1X, "x", lambda p: sx.at[it, p], rx.at[it]))
         value = grad(1)
         value_y = value[:, 0:128].reshape(NX, NY, 8, 128)
         value_z = value[:, 128:256].reshape(NX, NZ, 8, 128)
         for p in range(NY):
             sy[it, p] = value_y[:, p]
-        spread_out(stage + S1Y, "y", lambda p: sy.at[it, p], ry.at[it])
-        for p in range(NZ):
             sz[it, p] = value_z[:, p]
-        spread_out(stage + S1Z, "z", lambda p: sz.at[it, p], rz.at[it])
+        spread_out(
+            (stage + S1Y, "y", lambda p: sy.at[it, p], ry.at[it]),
+            (stage + S1Z, "z", lambda p: sz.at[it, p], rz.at[it]),
+        )
         rx[it, x] = sx[it, x]
         ry[it, y] = sy[it, y]
         rz[it, z] = sz[it, z]
@@ -220,7 +252,7 @@
         if it == 0:
             arrived(CSY, "y", csy)
             cst[z] = csy[z]
-            spread_out(CST, "z", lambda p: csy.at[p], cst)
+            spread_out((CST, "z", lambda p: csy.at[p], cst))
 
         arrived(stage + S1X, "x", rx.at[it])
         sum_x = summed(rx, NX)
@@ -228,10 +260,11 @@
             s2y[it, p, 0] = sum_x[p]
             s2y[it, p, 1] = sum_x[16]
             s2y[it, p, 2] = sum_x[17]
-        spread_out(stage + S2Y, "y", lambda p: s2y.at[it, p], r2y.at[it])
-        for p in range(NZ):
             s2z[it, p, 0] = sum_x[8 + p]
-        spread_out(stage + S2Z, "z", lambda p: s2z.at[it, p], r2z.at[it])
+        spread_out(
+            (stage + S2Y, "y", lambda p: s2y.at[it, p], r2y.at[it]),
+            (stage + S2Z, "z", lambda p: s2z.at[it, p], r2z.at[it]),
+        )
         r2y[it, y] = s2y[it, y]
         r2z[it, z] = s2z[it, z]
 
@@ -243,7 +276,7 @@
         sum_z = summed(rz, NZ)
         for p in range(NX):
             s2x[it, p, 1] = sum_z[p]
-        spread_out(stage + S2X, "x", lambda p: s2x.at[it, p], r2x.at[it])
+        spread_out((stage + S2X, "x", lambda p: s2x.at[it, p], r2x.at[it]))
         r2x[it, x] = s2x[it, x]
 
         arrived(stage + S2Y, "y", r2y.at[it])
@@ -257,8 +290,10 @@
         from_x = summed(r2x, NX)
         s3z[it, 1] = from_x[0]
         s3y[it, 1] = from_x[1]
-        spread_out(stage + S3Z, "z", lambda p: s3z.at[it], r3z.at[it])
-        spread_out(stage + S3Y, "y", lambda p: s3y.at[it], r3y.at[it])
+        spread_out(
+            (stage + S3Z, "z", lambda p: s3z.at[it], r3z.at[it]),
+            (stage + S3Y, "y", lambda p: s3y.at[it], r3y.at[it]),
+        )
         r3z[it, z] = s3z[it]
         r3y[it, y] = s3y[it]
         arrived(stage + S3Z, "z", r3z.at[it])
@@ -276,9 +311,11 @@
         a2z[it, 1] = grads[1] * grads[1] + grads[3] * grads[3]
         a2x[it, 0] = scales[2] * grads[2]
         a2x[it, 1] = scales[3] * grads[3]
-        spread_out(stage + A2Y, "y", lambda p: a2y.at[it], g2y.at[it])
-        spread_out(stage + A2Z, "z", lambda p: a2z.at[it], g2z.at[it])
-        spread_out(stage + A2X, "x", lambda p: a2x.at[it], g2x.at[it])
+        spread_out(
+            (stage + A2Y, "y", lambda p: a2y.at[it], g2y.at[it]),
+            (stage + A2Z, "z", lambda p: a2z.at[it], g2z.at[it]),
+            (stage + A2X, "x", lambda p: a2x.at[it], g2x.at[it]),
+        )
         g2y[it, y] = a2y[it]
         g2z[it, z] = a2z[it]
         g2x[it, x] = a2x[it]
@@ -291,13 +328,15 @@
             term = g2y[it, p, 1] + g2z[it, p, 1]
             square = term if square is None else square + term
         a1x[it, 16] = square
-        spread_out(stage + A1X, "x", lambda p: a1x.at[it], gx.at[it])
+        spread_out((stage + A1X, "x", lambda p: a1x.at[it], gx.at[it]))
         arrived(stage + A2X, "x", g2x.at[it])
         for p in range(NX):
             gy[it, y, p] = g2x[it, p, 0]
             gz[it, z, p] = g2x[it, p, 1]
-        spread_out(stage + A1Y, "y", lambda p: gy.at[it, y], gy.at[it])
-        spread_out(stage + A1Z, "z", lambda p: gz.at[it, z], gz.at[it])
+        spread_out(
+            (stage + A1Y, "y", lambda p: gy.at[it, y], gy.at[it]),
+            (stage + A1Z, "z", lambda p: gz.at[it, z], gz.at[it]),
+        )
         gx[it, x] = a1x[it]
         arrived(stage + A1X, "x", gx.at[it])
         square = gx[it, 0, 16]
@@ -339,9 +378,10 @@
         )
         ex[it, c] = jnp.zeros((4, 8, 128), F32)
         for k in range(2):
-            column = jnp.sum(sums[k], axis=1, keepdims=True)
+            column = jnp.sum(sums[k].reshape(32, 8, 128), axis=1)
+            column = jnp.sum(column, axis=1, keepdims=True)
             ex[it, c, 0, k : k + 1, 0:32] = jnp.sum(
-                jnp.where(ray_of, column, 0.0), axis=0, keepdims=True
+                jnp.where(eye32, column, 0.0), axis=0, keepdims=True
             )
         ex[it, c, 1] = square
         if it == 1:
@@ -414,18 +454,14 @@
     raw = [
         keeps[k] * (product[k] / alpha1 + at_station[k]) - alpha1 * unit[k] for k in range(2)
     ]
-    fin[...] = jnp.zeros((3, 8, 128), F32)
+    fin[...] = jnp.zeros((2, 8, 128), F32)
     fin[0, 0:1, 0:32] = raw[0] * raw[0] + raw[1] * raw[1]
-    spread_out(FX, "x", lambda p: fin.at[0], fx)
-    fx[x] = fin[0]
-    arrived(FX, "x", fx)
-    fin[1] = jnp.sum(fx[...], axis=0)
-    spread_out(FY, "y", lambda p: fin.at[1], fy)
-    fy[y] = fin[1]
-    arrived(FY, "y", fy)
-    fin[2] = jnp.sum(fy[...], axis=0)
-    spread_out(FZ, "z", lambda p: fin.at[2], fz)
-    fz[z] = fin[2]
+    spread_out((FW, "xy", lambda p: fin.at[0], fw))
+    fw[x * NY + y] = fin[0]
+    arrived(FW, "xy", fw)
+    fin[1] = jnp.sum(fw[...], axis=0)
+    spread_out((FZ, "z", lambda p: fin.at[1], fz))
+    fz[z] = fin[1]
     arrived(FZ, "z", fz)
     beta2 = jnp.sqrt(total(jnp.sum(fz[...], axis=0)) + EPS)
     rho = jnp.sqrt(rho_bar * rho_bar + beta2 * beta2)
@@ -448,6 +484,19 @@
         ).wait_send()
 
 
+def hand_out(model, station, ray, out_model, out_station, out_ray, sem):
+    copies = [
+        pltpu.make_async_copy(src, dst, sem.at[i])
+        for i, (src, dst) in enumerate(
+            ((model, out_model), (station, out_station), (ray, out_ray))
+        )
+    ]
+    for copy in copies:
+        copy.start()
+    for copy in copies:
+        copy.wait()
+
+
 def per_device(sensitivity, owners, local_block, station_ids, kept, times, hit_counts):
     vmem = pl.BlockSpec(memory_space=pltpu.VMEM)
 
@@ -461,7 +510,7 @@
             jax.ShapeDtypeStruct((8, 128), F32),
             jax.ShapeDtypeStruct((1, 32), F32),
         ),
-        in_specs=[pl.BlockSpec(memory_space=pl.ANY)] + [vmem] * 6,
+        in_specs=[pl.BlockSpec(memory_space=pltpu.HBM)] * 7,
         out_specs=(vmem,) * 3,
         scratch_shapes=[
             pltpu.VMEM((2, 32, 8, 512), F32),
@@ -469,7 +518,7 @@
             pltpu.VMEM((2, 256, 256), BF16),
             pltpu.VMEM((2, 256, 256), BF16),
             tiles(), tiles(NZ), tiles(NY), tiles(NZ),
-            tiles(3), tiles(NX), tiles(NY), tiles(NZ),
+            tiles(2), tiles(NX * NY), tiles(NZ),
             tiles(2, NX, 18), tiles(2, NY, 4), tiles(2, NZ, 4),
             tiles(2, NX, 18), tiles(2, NY, 4), tiles(2, NZ, 4),
             tiles(2, NY, 3), tiles(2, NZ, 1), tiles(2, NX, 2),
@@ -479,17 +528,28 @@
             tiles(2, NY, 2), tiles(2, NZ, 2), tiles(2, NX, 2),
             tiles(2, 17), tiles(2, NX, 17), tiles(2, NY, 4), tiles(2, NZ, 4),
             tiles(2, 2, 4),
-            pltpu.SemaphoreType.DMA,
+            pltpu.VMEM((8, 32), jnp.int32), pltpu.VMEM((8, 32), jnp.int32),
+            pltpu.VMEM((1, 32), jnp.int32), pltpu.VMEM((1, 32), jnp.int32),
+            pltpu.VMEM((1, 32), F32), pltpu.VMEM((1, 4, 128), jnp.int32),
+            pltpu.SemaphoreType.DMA((7,)),
             pltpu.SemaphoreType.DMA((STAGES,)),
             pltpu.SemaphoreType.DMA((STAGES,)),
         ],
         compiler_params=pltpu.CompilerParams(
-            collective_id=0, has_side_effects=True, vmem_limit_bytes=40 * 1024 * 1024
+            collective_id=0, has_side_effects=True, vmem_limit_bytes=60 * 1024 * 1024
         ),
     )(
-        sensitivity, owners, local_block, station_ids.reshape(1, 32), kept.reshape(1, 32),
+        sensitivity, owners.T, local_block.T, station_ids.reshape(1, 32), kept.reshape(1, 32),
         times.reshape(1, 32), hit_counts,
     )
+    hbm = pl.BlockSpec(memory_space=pltpu.HBM)
+    model, station, ray = pl.pallas_call(
+        hand_out,
+        out_shape=tuple(jax.ShapeDtypeStruct(a.shape, F32) for a in (model, station, ray)),
+        in_specs=[hbm] * 3,
+        out_specs=(hbm,) * 3,
+        scratch_shapes=[pltpu.SemaphoreType.DMA((3,))],
+    )(model, station, ray)
     return model, station.reshape(1024), ray.reshape(32)
 
 

time: 95.9 us -> 87.6 us (0.913)
  local copies, waits for them, and re-layouts: 4.97 us -> 0 us
  Pallas kernels: 90 us -> 86.8 us
    unnamed x19 -> x0, local copies, waits for them, and re-layouts: 4.97 us -> none
    pallas_call x1, Pallas kernels: 90 us -> 85.5 us  [per_device(): pl.pallas_call(kernel, out_shape=(jax.ShapeDtypeStruct((1, 4, 128), F32),...]
    pallas_call x0 -> x1, Pallas kernels: none -> 1.33 us  [per_device(): pl.pallas_call(hand_out, out_shape=tuple((jax.ShapeDtypeStruct(a.shape, F...]
where the time goes in v2:
time: 87.6 us; the launch traced here: 87.5 us
  Pallas kernels  86.8 us (99%)
    pallas_call x1, Pallas kernels, per_device(): pl.pallas_call(kernel, out_shape=(jax.ShapeDtypeStruct((1, 4, 128), F32),...  85.5 us

profile of v2, /device:TPU:1, one launch (start us, length us, event | category | flops | bytes accessed | tf_op | source)
XLA Modules:
  0.0 87.5 jit_solution(12346714706180955547)
XLA Ops:
  0.6 85.5 %shard_map.94 = (f32[1,4,128]{2,1,0:T(4,128)}, f32[8,128]{1,0:T(8,128)}, f32[1,32]{1,0:T(1,128)}) custom-call(f32[32,8,1024]{2,1,0:T(8,128)} %sens.1, s32[8,32]{1,0:T(8,128)} %bitcast.7, s32[8,32]{1,0:T(8,128)} %bitcast.8, s32[1,32]{1,0:T(1,128)} %bitcast.9, s32[1,32]{1,0:T(1,128)} %bitcast.10, f32[1,32]{1,0:T(1,128)} %bitcast.11, s32[1,4,128]{2,1,0:T(4,128)} %hits_in.1), custom_call_target="tpu_custom_call" | custom-call | tf_op jit(solution)/shard_map/pallas_call | solution.py:506
  86.1 1.3 %shard_map.95 = (f32[1,4,128]{2,1,0:T(4,128)}, f32[8,128]{1,0:T(8,128)}, f32[1,32]{1,0:T(1,128)}) custom-call(f32[1,4,128]{2,1,0:T(4,128)} %get-tuple-element.9.model, f32[8,128]{1,0:T(8,128)} %get-tuple-element.10.station, f32[1,32]{1,0:T(1,128)} %get-tuple-element.11.ray), custom_call_target="tpu_custom_call" | custom-call | tf_op jit(solution)/shard_map/pallas_call | solution.py:546

commit v3 on v2

v3 whole, which is shorter than its diff:
```python
import functools

import jax
import jax.numpy as jnp
from jax import lax
from jax.experimental import pallas as pl
from jax.experimental.pallas import tpu as pltpu
from jax.sharding import PartitionSpec as P

NX, NY, NZ = 4, 8, 8
EPS = 1e-06
F32 = jnp.float32
BF16 = jnp.bfloat16
HIGHEST = lax.Precision.HIGHEST
MESH = pl.DeviceIdType.MESH

ROWS = 0
META, CSZ, CSY, CST, FY, FZ = range(8, 14)
S1Y, S1Z, S2Z, S2Y, A1Y, A1Z, EX = range(7)
FIRST = 14
STAGES = FIRST + 2 * 7


def iota(shape, dim):
    return lax.broadcasted_iota(jnp.int32, shape, dim)


def total(tile):
    return jnp.sum(jnp.sum(tile, axis=0, keepdims=True), axis=1, keepdims=True)


def split(value):
    high = value.astype(BF16)
    return jnp.concatenate([high, (value - high.astype(F32)).astype(BF16)], axis=1)


def joined(value):
    return value[:, 0:128] + value[:, 128:256]


def dot(a, b):
    return jnp.dot(a, b, preferred_element_type=F32)


def dot_exact(a, b):
    return jnp.dot(a, b, precision=HIGHEST, preferred_element_type=F32)


def dot_nt(a, b):
    return lax.dot_general(
        a, b, (((1,), (1,)), ((), ())), precision=HIGHEST, preferred_element_type=F32
    )


def kernel(
    sens, owners_in, local_in, station_in, kept_in, times_in, hits_in,
    out_model, out_station, out_ray,
    rows, meta, ohr, ohc, cs_near, csz, csy, cst, fin, fy, fz,
    sy, sz, ry, rz, s2z, s2y, r2z, r2y, a1y, a1z, gy, gz, exs, ex,
    owners, local_block, station_ids, kept, times, hits, local_sem, send_sem, recv_sem,
):
    z = lax.axis_index("depth")
    b = lax.axis_index("block")
    c = lax.rem(b, 2)
    y = lax.rem(lax.div(b, 2), NY)
    x = lax.div(b, 2 * NY)
    q = x * 2 + c
    axes = {
        "y": (NY, y, lambda p: (z, (x * NY + p) * 2 + c)),
        "z": (NZ, z, lambda p: (p, b)),
        "g": (2 * NX, q, lambda p: (z, (lax.div(p, 2) * NY + y) * 2 + lax.rem(p, 2))),
    }

    def member(step, sign=1):
        return lax.rem(x + sign * (step // 2) + NX, NX) * 2 + lax.rem(c + step, 2)

    fetches = [
        pltpu.make_async_copy(src, dst, local_sem.at[i])
        for i, (src, dst) in enumerate(
            (
                (owners_in, owners),
                (local_in, local_block),
                (station_in, station_ids),
                (kept_in, kept),
                (times_in, times),
                (hits_in, hits),
            )
        )
    ]
    for fetch in fetches:
        fetch.start()

    def layer_of_rows(p):
        return sens.at[:, :, pl.ds(pl.multiple_of(p * 128, 128), 128)]

    own_rows = pltpu.make_async_copy(layer_of_rows(q), rows.at[q], local_sem.at[6])
    own_rows.start()

    barrier = pltpu.get_barrier_semaphore()
    for name in "yz":
        n, me, peer = axes[name]
        for step in (4, 3, 5, 2, 6, 1, 7):
            pl.semaphore_signal(
                barrier, inc=1, device_id=peer(lax.rem(me + step, n)), device_id_type=MESH
            )
    for step in (4, 5, 2, 3, 6, 7, 1):
        pl.semaphore_signal(
            barrier, inc=1, device_id=axes["g"][2](member(step)), device_id_type=MESH
        )
    for fetch in fetches:
        fetch.wait()

    blocks = (owners[...] * 4 + local_block[...]).astype(F32)
    widen = (lax.shift_right_logical(iota((32, 256), 1), 3) == iota((32, 256), 0)).astype(F32)
    by_slot = dot_exact(blocks, widen)
    slot_of = jnp.bitwise_and(iota((8, 256), 1), 7)
    block_row = jnp.sum(
        jnp.where(iota((8, 256), 0) == slot_of, by_slot, 0.0), axis=0, keepdims=True
    )
    keep = kept[...].astype(F32)
    kind = iota((8, 32), 0)
    stacked = jnp.where(
        kind < 4, keep * times[...], jnp.where(kind < 6, keep, station_ids[...].astype(F32))
    )
    repeat = (jnp.bitwise_and(iota((32, 128), 1), 31) == iota((32, 128), 0)).astype(F32)
    mine = jnp.logical_and(
        lax.shift_right_logical(iota((8, 128), 1), 5) == lax.rem(q, 4),
        jnp.bitwise_and(iota((8, 128), 0), 1) == lax.div(q, 4),
    )
    scale = 1.0 / jnp.sqrt(1.0 + hits[0].astype(F32))
    meta[q, 0] = jnp.where(mine, dot_exact(stacked, repeat), 0.0)
    meta[q, 0, 0:1, :] = block_row[:, 0:128]
    meta[q, 0, 1:2, :] = block_row[:, 128:256]
    meta[q, 1, 0:4, :] = jnp.where(c == 0, scale, 0.0)
    meta[q, 1, 4:8, :] = jnp.where(c == 1, scale, 0.0)

    pl.semaphore_wait(barrier, 7 + (NY - 1) + (NZ - 1))

    pending = []

    def send(stage, src, dst, device):
        copy = pltpu.make_async_remote_copy(
            src_ref=src, dst_ref=dst, send_sem=send_sem.at[stage], recv_sem=recv_sem.at[stage],
            device_id=device, device_id_type=MESH,
        )
        copy.start()
        return copy

    def spread_out(*parts):
        sends = []
        for stage, name, source, buffer in parts:
            n, me, peer = axes[name]
            for step in range(1, n):
                away = min(step, n - step)
                if name == "g":
                    away = min(step // 2, NX - step // 2)
                sends.append((-away, len(sends), stage, name, source, buffer, step))
            pending.append((stage, buffer.at[pl.ds(0, n - 1)]))
        for away, order, stage, name, source, buffer, step in sorted(sends, key=lambda t: t[:2]):
            n, me, peer = axes[name]
            p = member(step) if name == "g" else lax.rem(me + step, n)
            send(stage, source(p), buffer.at[me], peer(p))

    def arrived(stage, name, buffer):
        n, me, peer = axes[name]
        others = buffer.at[pl.ds(0, n - 1)]
        pltpu.make_async_remote_copy(
            src_ref=others, dst_ref=others, send_sem=send_sem.at[stage],
            recv_sem=recv_sem.at[stage], device_id=peer(lax.rem(me + 1, n)), device_id_type=MESH,
        ).wait_recv()

    spread_out((META, "g", lambda p: meta.at[q], meta))
    row_copies = {}
    for step in (1, 4, 5, 2, 3, 6, 7):
        p = member(step)
        row_copies[step] = send(ROWS + step, layer_of_rows(p), rows.at[q], axes["g"][2](p))
    arrived(META, "g", meta)

    for i in range(NX):
        cs_near[i] = meta[2 * i, 1] + meta[2 * i + 1, 1]
    csz[z] = cs_near[0:2]
    csy[y] = cs_near[2:4]
    spread_out(
        (CSY, "y", lambda p: cs_near.at[pl.ds(2, 2)], csy),
        (CSZ, "z", lambda p: cs_near.at[pl.ds(0, 2)], csz),
    )

    packed = meta[0, 0]
    for k in range(1, 8):
        packed = packed + meta[k, 0]
    raw = [packed[2 + h : 3 + h] for h in range(2)]
    keeps = [packed[4 + h : 5 + h] for h in range(2)]
    ids = [packed[6 + h : 7 + h].astype(jnp.int32) for h in range(2)]
    station_high = [
        lax.shift_right_logical(ids[h], 7) == iota((8, 128), 0) for h in range(2)
    ]
    station_low = [
        (jnp.bitwise_and(ids[h], 127) == iota((128, 128), 0)).astype(F32) for h in range(2)
    ]
    sub = iota((256, 128), 0)
    lane = iota((256, 128), 1)
    for k in range(8):
        column = jnp.zeros((256, 1), F32)
        for h in range(2):
            part = meta[k, 0, h : h + 1, :]
            ohr[k, :, 128 * h : 128 * h + 128] = (
                jnp.where(part == sub.astype(F32), 1.0, 0.0).astype(BF16)
            )
            column += jnp.sum(
                jnp.where(sub == lane + 128 * h, part, 0.0), axis=1, keepdims=True
            )
        for h in range(2):
            ohc[k, :, 128 * h : 128 * h + 128] = (
                jnp.where(column == (lane + 128 * h).astype(F32), 1.0, 0.0).astype(BF16)
            )

    def lanes_of(k):
        return iota((32, 128), 1) == iota((32, 128), 0) + 32 * lax.rem(k, 4)

    def column_of(k, ray):
        half = jnp.where(k < 4, ray[0], ray[1])
        return jnp.sum(jnp.where(lanes_of(k), half, 0.0), axis=1, keepdims=True)

    def summed(buffer, it, n):
        result = buffer[it, 0]
        for p in range(1, n):
            result = result + buffer[it, p]
        return result

    def adjoint_and_reduce(it, ray):
        stage = FIRST + 7 * it
        stations = jnp.zeros((8, 128), F32)
        for h in range(2):
            stations += dot_nt(jnp.where(station_high[h], ray[h], 0.0), station_low[h])
        for p in range(NY):
            sy[it, p, 2] = stations
            sy[it, p, 3] = jnp.zeros((8, 128), F32)
            for h in range(2):
                sy[it, p, 3, h : h + 1, :] = ray[h] * ray[h]
        value = None
        for step in (0, 1, 2, 3, 6, 7, 4, 5):
            k = member(step, -1)
            if it == 0:
                if step:
                    row_copies[step].wait_recv()
                else:
                    own_rows.wait()
            column = jnp.broadcast_to(column_of(k, ray), (32, 128)).reshape(32, 1, 128)
            term = dot(ohr[k], split((rows[k] * column).reshape(256, 128)))
            value = term if value is None else value + term
        value = joined(value).reshape(NX, NY, 8, 128)
        for p in range(NY):
            for i in range(2):
                sy[it, p, i] = value[i, p]
                sz[it, p, i] = value[2 + i, p]
        spread_out(
            (stage + S1Y, "y", lambda p: sy.at[it, p], ry.at[it]),
            (stage + S1Z, "z", lambda p: sz.at[it, p], rz.at[it]),
        )
        ry[it, y] = sy[it, y]
        rz[it, z] = sz[it, z]
        if it == 0:
            arrived(CSY, "y", csy)
            cst[z] = csy[z]
            spread_out((CST, "z", lambda p: csy.at[p], cst))
        arrived(stage + S1Y, "y", ry.at[it])
        s2z[it] = summed(ry, it, NY)
        spread_out((stage + S2Z, "z", lambda p: s2z.at[it], r2z.at[it]))
        arrived(stage + S1Z, "z", rz.at[it])
        s2y[it] = summed(rz, it, NZ)
        spread_out((stage + S2Y, "y", lambda p: s2y.at[it], r2y.at[it]))
        r2z[it, z] = s2z[it]
        r2y[it, y] = s2y[it]
        arrived(stage + S2Z, "z", r2z.at[it])
        from_z = summed(r2z, it, NZ)
        arrived(stage + S2Y, "y", r2y.at[it])
        from_y = summed(r2y, it, NY)
        return [from_z[0:2], from_y], from_z[2], jnp.sqrt(total(from_z[3]) + EPS)

    def gather(it, grads, scales):
        stage = FIRST + 7 * it
        for buffer, grad, scale in ((a1y, grads[0], scales[0]), (a1z, grads[1], scales[1])):
            buffer[it, 0:2] = scale * grad
            buffer[it, 2] = grad[0] * grad[0] + grad[1] * grad[1]
        spread_out(
            (stage + A1Y, "y", lambda p: a1y.at[it], gy.at[it]),
            (stage + A1Z, "z", lambda p: a1z.at[it], gz.at[it]),
        )
        gy[it, y] = a1y[it]
        gz[it, z] = a1z[it]

    def forward(it):
        stage = FIRST + 7 * it
        arrived(stage + A1Y, "y", gy.at[it])
        arrived(stage + A1Z, "z", gz.at[it])
        values = split(
            jnp.concatenate(
                [buffer[it, :, i].reshape(64, 128) for buffer in (gy, gz) for i in range(2)],
                axis=0,
            )
        )
        halves = [jnp.zeros((1, 128), F32), jnp.zeros((1, 128), F32)]
        for k in range(8):
            part = rows[k].reshape(256, 128) * joined(dot(ohc[k], values))
            column = jnp.sum(part.reshape(32, 8, 128), axis=1)
            column = jnp.sum(column, axis=1, keepdims=True)
            halves[k // 4] += jnp.sum(jnp.where(lanes_of(k), column, 0.0), axis=0, keepdims=True)
        square = gy[it, 0, 2] + gz[it, 0, 2]
        for p in range(1, NY):
            square = square + (gy[it, p, 2] + gz[it, p, 2])
        for p in range(8):
            exs[it, p, 0] = jnp.zeros((8, 128), F32)
            for h in range(2):
                exs[it, p, 0, h : h + 1, :] = halves[h]
            exs[it, p, 1] = square
            for i in range(2):
                if it == 1:
                    exs[it, p, 2 + i] = (gy if p < 4 else gz)[i, y, p // 2 % 2]
        width = 4 if it == 1 else 2
        spread_out(
            (
                stage + EX,
                "g",
                lambda p: exs.at[it, p, pl.ds(0, width)],
                ex.at[it, :, pl.ds(0, width)],
            )
        )
        ex[it, q, 0:width] = exs[it, q, 0:width]
        arrived(stage + EX, "g", ex.at[it, :, pl.ds(0, width)])
        value = ex[it, 0, 0:2]
        for k in range(1, 8):
            value = value + ex[it, k, 0:2]
        return [value[0, h : h + 1] for h in range(2)], total(value[1])

    def station_values(stations):
        return [
            jnp.sum(
                jnp.where(station_high[h], dot_exact(stations, station_low[h]), 0.0),
                axis=0,
                keepdims=True,
            )
            for h in range(2)
        ]

    sums, station_sum, beta0 = adjoint_and_reduce(0, raw)
    unit = [raw[h] / beta0 for h in range(2)]
    arrived(CSZ, "z", csz)
    arrived(CST, "z", cst)
    scales = [csz[q], cst[q]]
    grads0 = [scales[j] * sums[j] / beta0 for j in range(2)]
    grad_station0 = station_sum / beta0
    gather(0, grads0, scales)
    product, model_square = forward(0)
    alpha0 = jnp.sqrt(model_square + total(grad_station0 * grad_station0) + EPS)
    dir_station0 = grad_station0 / alpha0

    at_station = station_values(dir_station0)
    raw = [
        keeps[h] * (product[h] / alpha0 + at_station[h]) - alpha0 * unit[h] for h in range(2)
    ]
    sums, station_sum, beta1 = adjoint_and_reduce(1, raw)
    unit = [raw[h] / beta1 for h in range(2)]
    grads1 = [scales[j] * sums[j] / beta1 - beta1 * (grads0[j] / alpha0) for j in range(2)]
    grad_station1 = station_sum / beta1 - beta1 * dir_station0
    gather(1, grads1, scales)
    product, model_square = forward(1)
    alpha1 = jnp.sqrt(model_square + total(grad_station1 * grad_station1) + EPS)
    dir_station1 = grad_station1 / alpha1
    rho = jnp.sqrt(alpha0 * alpha0 + beta1 * beta1)
    cosine = alpha0 / rho
    sine = beta1 / rho
    theta = sine * alpha1
    rho_bar = -cosine * alpha1
    step0 = cosine * beta0 / rho
    phi_bar = sine * beta0
    turn = theta / rho

    at_station = station_values(dir_station1)
    raw = [
        keeps[h] * (product[h] / alpha1 + at_station[h]) - alpha1 * unit[h] for h in range(2)
    ]
    fin[...] = jnp.zeros((2, 8, 128), F32)
    for h in range(2):
        fin[0, h : h + 1, :] = raw[h] * raw[h]
    spread_out((FY, "y", lambda p: fin.at[0], fy))
    fy[y] = fin[0]
    arrived(FY, "y", fy)
    fin[1] = jnp.sum(fy[...], axis=0)
    spread_out((FZ, "z", lambda p: fin.at[1], fz))
    fz[z] = fin[1]
    own_ray = jnp.sum(
        jnp.where(iota((32, 32), 0) == iota((32, 32), 1), column_of(q, raw), 0.0),
        axis=0,
        keepdims=True,
    )
    arrived(FZ, "z", fz)
    beta2 = jnp.sqrt(total(jnp.sum(fz[...], axis=0)) + EPS)
    rho = jnp.sqrt(rho_bar * rho_bar + beta2 * beta2)
    step1 = rho_bar / rho * phi_bar / rho

    weight0 = (step0 - step1 * turn) / alpha0
    weight1 = step1 / alpha1
    model = weight0 * ex[1, z, 2] + weight1 * ex[1, z, 3]
    out_model[0] = jnp.where(c == 0, model[0:4], model[4:8])
    out_station[...] = (step0 - step1 * turn) * dir_station0 + step1 * dir_station1
    out_ray[...] = own_ray / beta2

    for step in row_copies:
        row_copies[step].wait_send()
    for stage, others in pending:
        pltpu.make_async_remote_copy(
            src_ref=others, dst_ref=others, send_sem=send_sem.at[stage],
            recv_sem=recv_sem.at[stage], device_id=axes["g"][2](member(1)), device_id_type=MESH,
        ).wait_send()


def hand_out(model, station, ray, out_model, out_station, out_ray, sem):
    copies = [
        pltpu.make_async_copy(src, dst, sem.at[i])
        for i, (src, dst) in enumerate(
            ((model, out_model), (station, out_station), (ray, out_ray))
        )
    ]
    for copy in copies:
        copy.start()
    for copy in copies:
        copy.wait()


def per_device(sensitivity, owners, local_block, station_ids, kept, times, hit_counts):
    vmem = pl.BlockSpec(memory_space=pltpu.VMEM)

    def tiles(*shape):
        return pltpu.VMEM(shape + (8, 128), F32)

    model, station, ray = pl.pallas_call(
        kernel,
        out_shape=(
            jax.ShapeDtypeStruct((1, 4, 128), F32),
            jax.ShapeDtypeStruct((8, 128), F32),
            jax.ShapeDtypeStruct((1, 32), F32),
        ),
        in_specs=[pl.BlockSpec(memory_space=pltpu.HBM)] * 7,
        out_specs=(vmem,) * 3,
        scratch_shapes=[
            pltpu.VMEM((8, 32, 8, 128), F32),
            tiles(8, 2),
            pltpu.VMEM((8, 256, 256), BF16),
            pltpu.VMEM((8, 256, 256), BF16),
            tiles(NX), tiles(NZ, 2), tiles(NY, 2), tiles(NZ, 2),
            tiles(2), tiles(NY), tiles(NZ),
            tiles(2, NY, 4), tiles(2, NZ, 2), tiles(2, NY, 4), tiles(2, NZ, 2),
            tiles(2, 4), tiles(2, 2), tiles(2, NZ, 4), tiles(2, NY, 2),
            tiles(2, 3), tiles(2, 3), tiles(2, NY, 3), tiles(2, NZ, 3),
            tiles(2, 8, 4), tiles(2, 8, 4),
            pltpu.VMEM((8, 32), jnp.int32), pltpu.VMEM((8, 32), jnp.int32),
            pltpu.VMEM((1, 32), jnp.int32), pltpu.VMEM((1, 32), jnp.int32),
            pltpu.VMEM((1, 32), F32), pltpu.VMEM((1, 4, 128), jnp.int32),
            pltpu.SemaphoreType.DMA((7,)),
            pltpu.SemaphoreType.DMA((STAGES,)),
            pltpu.SemaphoreType.DMA((STAGES,)),
        ],
        compiler_params=pltpu.CompilerParams(
            collective_id=0, has_side_effects=True, vmem_limit_bytes=60 * 1024 * 1024
        ),
    )(
        sensitivity, owners.T, local_block.T, station_ids.reshape(1, 32), kept.reshape(1, 32),
        times.reshape(1, 32), hit_counts,
    )
    hbm = pl.BlockSpec(memory_space=pltpu.HBM)
    model, station, ray = pl.pallas_call(
        hand_out,
        out_shape=tuple(jax.ShapeDtypeStruct(a.shape, F32) for a in (model, station, ray)),
        in_specs=[hbm] * 3,
        out_specs=(hbm,) * 3,
        scratch_shapes=[pltpu.SemaphoreType.DMA((3,))],
    )(model, station, ray)
    return model, station.reshape(1024), ray.reshape(32)


def solution(mesh):
    in_specs = (
        P(("depth", "block"), None, None),
        P(("depth", "block"), None),
        P(("depth", "block"), None),
        P(("depth", "block")),
        P(("depth", "block")),
        P(("depth", "block")),
        P("depth", "block", None),
    )
    out_specs = (P("depth", "block", None), P(), P(("depth", "block")))
    return jax.shard_map(
        per_device, mesh=mesh, in_specs=in_specs, out_specs=out_specs, check_vma=False
    )
```

time: 87.6 us -> 82.4 us (0.941)
  Pallas kernels: 86.8 us -> 81.5 us
    pallas_call x1, Pallas kernels: 85.5 us -> 80.1 us  [per_device(): pl.pallas_call(kernel, out_shape=(jax.ShapeDtypeStruct((1, 4, 128), F32),...]
where the time goes in v3:
time: 82.4 us; the launch traced here: 82.1 us
  Pallas kernels  81.5 us (99%)
    pallas_call x1, Pallas kernels, per_device(): pl.pallas_call(kernel, out_shape=(jax.ShapeDtypeStruct((1, 4, 128), F32),...  80.1 us

profile of v3, /device:TPU:1, one launch (start us, length us, event | category | flops | bytes accessed | tf_op | source)
XLA Modules:
  0.0 82.1 jit_solution(5840775878539416818)
XLA Ops:
  0.6 80.1 %shard_map.94 = (f32[1,4,128]{2,1,0:T(4,128)}, f32[8,128]{1,0:T(8,128)}, f32[1,32]{1,0:T(1,128)}) custom-call(f32[32,8,1024]{2,1,0:T(8,128)} %sens.1, s32[8,32]{1,0:T(8,128)} %bitcast.7, s32[8,32]{1,0:T(8,128)} %bitcast.8, s32[1,32]{1,0:T(1,128)} %bitcast.9, s32[1,32]{1,0:T(1,128)} %bitcast.10, f32[1,32]{1,0:T(1,128)} %bitcast.11, s32[1,4,128]{2,1,0:T(4,128)} %hits_in.1), custom_call_target="tpu_custom_call" | custom-call | tf_op jit(solution)/shard_map/pallas_call | solution.py:436
  80.8 1.3 %shard_map.95 = (f32[1,4,128]{2,1,0:T(4,128)}, f32[8,128]{1,0:T(8,128)}, f32[1,32]{1,0:T(1,128)}) custom-call(f32[1,4,128]{2,1,0:T(4,128)} %get-tuple-element.9.model, f32[8,128]{1,0:T(8,128)} %get-tuple-element.10.station, f32[1,32]{1,0:T(1,128)} %get-tuple-element.11.ray), custom_call_target="tpu_custom_call" | custom-call | tf_op jit(solution)/shard_map/pallas_call | solution.py:471

commit v4 on v3

--- a/solution.py
+++ b/solution.py
@@ -55,7 +55,7 @@
 def kernel(
     sens, owners_in, local_in, station_in, kept_in, times_in, hits_in,
     out_model, out_station, out_ray,
-    rows, meta, ohr, ohc, cs_near, csz, csy, cst, fin, fy, fz,
+    rows, parcels, meta, ohr, ohc, cs_near, csz, csy, cst, fin, fy, fz,
     sy, sz, ry, rz, s2z, s2y, r2z, r2y, a1y, a1z, gy, gz, exs, ex,
     owners, local_block, station_ids, kept, times, hits, local_sem, send_sem, recv_sem,
 ):
@@ -95,6 +95,12 @@
 
     own_rows = pltpu.make_async_copy(layer_of_rows(q), rows.at[q], local_sem.at[6])
     own_rows.start()
+    packings = [
+        pltpu.make_async_copy(layer_of_rows(p), parcels.at[p], local_sem.at[7 + p])
+        for p in range(8)
+    ]
+    for packing in packings:
+        packing.start()
 
     barrier = pltpu.get_barrier_semaphore()
     for name in "yz":
@@ -107,7 +113,7 @@
         pl.semaphore_signal(
             barrier, inc=1, device_id=axes["g"][2](member(step)), device_id_type=MESH
         )
-    for fetch in fetches:
+    for fetch in fetches + packings:
         fetch.wait()
 
     blocks = (owners[...] * 4 + local_block[...]).astype(F32)
@@ -171,9 +177,9 @@
 
     spread_out((META, "g", lambda p: meta.at[q], meta))
     row_copies = {}
-    for step in (1, 4, 5, 2, 3, 6, 7):
+    for step in (1, 2, 6, 3, 7, 4, 5):
         p = member(step)
-        row_copies[step] = send(ROWS + step, layer_of_rows(p), rows.at[q], axes["g"][2](p))
+        row_copies[step] = send(ROWS + step, parcels.at[p], rows.at[q], axes["g"][2](p))
     arrived(META, "g", meta)
 
     for i in range(NX):
@@ -444,6 +450,7 @@
         out_specs=(vmem,) * 3,
         scratch_shapes=[
             pltpu.VMEM((8, 32, 8, 128), F32),
+            pltpu.VMEM((8, 32, 8, 128), F32),
             tiles(8, 2),
             pltpu.VMEM((8, 256, 256), BF16),
             pltpu.VMEM((8, 256, 256), BF16),
@@ -456,7 +463,7 @@
             pltpu.VMEM((8, 32), jnp.int32), pltpu.VMEM((8, 32), jnp.int32),
             pltpu.VMEM((1, 32), jnp.int32), pltpu.VMEM((1, 32), jnp.int32),
             pltpu.VMEM((1, 32), F32), pltpu.VMEM((1, 4, 128), jnp.int32),
-            pltpu.SemaphoreType.DMA((7,)),
+            pltpu.SemaphoreType.DMA((15,)),
             pltpu.SemaphoreType.DMA((STAGES,)),
             pltpu.SemaphoreType.DMA((STAGES,)),
         ],

time: 82.4 us -> 82 us (level)
  no operation moved by 1% of the time
where the time goes in v4:
time: 82 us; the launch traced here: 81.9 us
  Pallas kernels  81.2 us (99%)
    pallas_call x1, Pallas kernels, per_device(): pl.pallas_call(kernel, out_shape=(jax.ShapeDtypeStruct((1, 4, 128), F32),...  79.9 us

profile of v4, /device:TPU:1, one launch (start us, length us, event | category | flops | bytes accessed | tf_op | source)
XLA Modules:
  0.0 81.9 jit_solution(2804758911250205358)
XLA Ops:
  0.6 79.9 %shard_map.94 = (f32[1,4,128]{2,1,0:T(4,128)}, f32[8,128]{1,0:T(8,128)}, f32[1,32]{1,0:T(1,128)}) custom-call(f32[32,8,1024]{2,1,0:T(8,128)} %sens.1, s32[8,32]{1,0:T(8,128)} %bitcast.7, s32[8,32]{1,0:T(8,128)} %bitcast.8, s32[1,32]{1,0:T(1,128)} %bitcast.9, s32[1,32]{1,0:T(1,128)} %bitcast.10, f32[1,32]{1,0:T(1,128)} %bitcast.11, s32[1,4,128]{2,1,0:T(4,128)} %hits_in.1), custom_call_target="tpu_custom_call" | custom-call | tf_op jit(solution)/shard_map/pallas_call | solution.py:442
  80.5 1.3 %shard_map.95 = (f32[1,4,128]{2,1,0:T(4,128)}, f32[8,128]{1,0:T(8,128)}, f32[1,32]{1,0:T(1,128)}) custom-call(f32[1,4,128]{2,1,0:T(4,128)} %get-tuple-element.9.model, f32[8,128]{1,0:T(8,128)} %get-tuple-element.10.station, f32[1,32]{1,0:T(1,128)} %get-tuple-element.11.ray), custom_call_target="tpu_custom_call" | custom-call | tf_op jit(solution)/shard_map/pallas_call | solution.py:478

commit v5 on v4

--- a/solution.py
+++ b/solution.py
@@ -74,6 +74,17 @@
     def member(step, sign=1):
         return lax.rem(x + sign * (step // 2) + NX, NX) * 2 + lax.rem(c + step, 2)
 
+    barrier = pltpu.get_barrier_semaphore()
+    for name in "yz":
+        n, me, peer = axes[name]
+        for step in (4, 3, 5, 2, 6, 1, 7):
+            pl.semaphore_signal(
+                barrier, inc=1, device_id=peer(lax.rem(me + step, n)), device_id_type=MESH
+            )
+    for step in (4, 5, 2, 3, 6, 7, 1):
+        pl.semaphore_signal(
+            barrier, inc=1, device_id=axes["g"][2](member(step)), device_id_type=MESH
+        )
     fetches = [
         pltpu.make_async_copy(src, dst, local_sem.at[i])
         for i, (src, dst) in enumerate(
@@ -102,17 +113,6 @@
     for packing in packings:
         packing.start()
 
-    barrier = pltpu.get_barrier_semaphore()
-    for name in "yz":
-        n, me, peer = axes[name]
-        for step in (4, 3, 5, 2, 6, 1, 7):
-            pl.semaphore_signal(
-                barrier, inc=1, device_id=peer(lax.rem(me + step, n)), device_id_type=MESH
-            )
-    for step in (4, 5, 2, 3, 6, 7, 1):
-        pl.semaphore_signal(
-            barrier, inc=1, device_id=axes["g"][2](member(step)), device_id_type=MESH
-        )
     for fetch in fetches + packings:
         fetch.wait()
 
@@ -295,7 +295,17 @@
         gy[it, y] = a1y[it]
         gz[it, z] = a1z[it]
 
-    def forward(it):
+    def station_values(stations):
+        return [
+            jnp.sum(
+                jnp.where(station_high[h], dot_exact(stations, station_low[h]), 0.0),
+                axis=0,
+                keepdims=True,
+            )
+            for h in range(2)
+        ]
+
+    def forward(it, stations):
         stage = FIRST + 7 * it
         arrived(stage + A1Y, "y", gy.at[it])
         arrived(stage + A1Z, "z", gz.at[it])
@@ -332,45 +342,54 @@
             )
         )
         ex[it, q, 0:width] = exs[it, q, 0:width]
+        at_station = station_values(stations)
+        station_square = total(stations * stations)
         arrived(stage + EX, "g", ex.at[it, :, pl.ds(0, width)])
         value = ex[it, 0, 0:2]
         for k in range(1, 8):
             value = value + ex[it, k, 0:2]
-        return [value[0, h : h + 1] for h in range(2)], total(value[1])
-
-    def station_values(stations):
-        return [
-            jnp.sum(
-                jnp.where(station_high[h], dot_exact(stations, station_low[h]), 0.0),
-                axis=0,
-                keepdims=True,
-            )
-            for h in range(2)
-        ]
+        return (
+            [value[0, h : h + 1] for h in range(2)], at_station, total(value[1]), station_square
+        )
 
     sums, station_sum, beta0 = adjoint_and_reduce(0, raw)
-    unit = [raw[h] / beta0 for h in range(2)]
     arrived(CSZ, "z", csz)
     arrived(CST, "z", cst)
     scales = [csz[q], cst[q]]
-    grads0 = [scales[j] * sums[j] / beta0 for j in range(2)]
+    grads0 = [scales[j] * sums[j] for j in range(2)]
+    gather(0, grads0, scales)
+    unit = [raw[h] / beta0 for h in range(2)]
     grad_station0 = station_sum / beta0
-    gather(0, grads0, scales)
-    product, model_square = forward(0)
-    alpha0 = jnp.sqrt(model_square + total(grad_station0 * grad_station0) + EPS)
+    over_beta0 = 1.0 / beta0
+    product, at_station, model_square, station_square = forward(0, grad_station0)
+    alpha0 = jnp.sqrt(model_square * over_beta0 * over_beta0 + station_square + EPS)
+    over0 = over_beta0 / alpha0
+
+    raw = [
+        keeps[h] * (product[h] * over0 + at_station[h] / alpha0) - alpha0 * unit[h]
+        for h in range(2)
+    ]
+    sums, station_sum, beta1 = adjoint_and_reduce(1, raw)
+    grads1 = [scales[j] * sums[j] / beta1 - beta1 * over0 * grads0[j] for j in range(2)]
+    gather(1, grads1, scales)
+    unit = [raw[h] / beta1 for h in range(2)]
     dir_station0 = grad_station0 / alpha0
-
-    at_station = station_values(dir_station0)
+    grad_station1 = station_sum / beta1 - beta1 * dir_station0
+    product, at_station, model_square, station_square = forward(1, grad_station1)
+    alpha1 = jnp.sqrt(model_square + station_square + EPS)
+
     raw = [
-        keeps[h] * (product[h] / alpha0 + at_station[h]) - alpha0 * unit[h] for h in range(2)
-    ]
-    sums, station_sum, beta1 = adjoint_and_reduce(1, raw)
-    unit = [raw[h] / beta1 for h in range(2)]
-    grads1 = [scales[j] * sums[j] / beta1 - beta1 * (grads0[j] / alpha0) for j in range(2)]
-    grad_station1 = station_sum / beta1 - beta1 * dir_station0
-    gather(1, grads1, scales)
-    product, model_square = forward(1)
-    alpha1 = jnp.sqrt(model_square + total(grad_station1 * grad_station1) + EPS)
+        keeps[h] * ((product[h] + at_station[h]) / alpha1) - alpha1 * unit[h] for h in range(2)
+    ]
+    fin[...] = jnp.zeros((2, 8, 128), F32)
+    for h in range(2):
+        fin[0, h : h + 1, :] = raw[h] * raw[h]
+    spread_out((FY, "y", lambda p: fin.at[0], fy))
+    fy[y] = fin[0]
+    arrived(FY, "y", fy)
+    fin[1] = jnp.sum(fy[...], axis=0)
+    spread_out((FZ, "z", lambda p: fin.at[1], fz))
+    fz[z] = fin[1]
     dir_station1 = grad_station1 / alpha1
     rho = jnp.sqrt(alpha0 * alpha0 + beta1 * beta1)
     cosine = alpha0 / rho
@@ -380,20 +399,6 @@
     step0 = cosine * beta0 / rho
     phi_bar = sine * beta0
     turn = theta / rho
-
-    at_station = station_values(dir_station1)
-    raw = [
-        keeps[h] * (product[h] / alpha1 + at_station[h]) - alpha1 * unit[h] for h in range(2)
-    ]
-    fin[...] = jnp.zeros((2, 8, 128), F32)
-    for h in range(2):
-        fin[0, h : h + 1, :] = raw[h] * raw[h]
-    spread_out((FY, "y", lambda p: fin.at[0], fy))
-    fy[y] = fin[0]
-    arrived(FY, "y", fy)
-    fin[1] = jnp.sum(fy[...], axis=0)
-    spread_out((FZ, "z", lambda p: fin.at[1], fz))
-    fz[z] = fin[1]
     own_ray = jnp.sum(
         jnp.where(iota((32, 32), 0) == iota((32, 32), 1), column_of(q, raw), 0.0),
         axis=0,
@@ -404,7 +409,7 @@
     rho = jnp.sqrt(rho_bar * rho_bar + beta2 * beta2)
     step1 = rho_bar / rho * phi_bar / rho
 
-    weight0 = (step0 - step1 * turn) / alpha0
+    weight0 = (step0 - step1 * turn) * over0
     weight1 = step1 / alpha1
     model = weight0 * ex[1, z, 2] + weight1 * ex[1, z, 3]
     out_model[0] = jnp.where(c == 0, model[0:4], model[4:8])

time: 82 us -> 81.6 us (level)
  no operation moved by 1% of the time
where the time goes in v5:
time: 81.6 us; the launch traced here: 81.4 us
  Pallas kernels  80.8 us (99%)
    pallas_call x1, Pallas kernels, per_device(): pl.pallas_call(kernel, out_shape=(jax.ShapeDtypeStruct((1, 4, 128), F32),...  79.5 us

profile of v5, /device:TPU:1, one launch (start us, length us, event | category | flops | bytes accessed | tf_op | source)
XLA Modules:
  0.0 81.4 jit_solution(16500724586007557499)
XLA Ops:
  0.6 79.5 %shard_map.94 = (f32[1,4,128]{2,1,0:T(4,128)}, f32[8,128]{1,0:T(8,128)}, f32[1,32]{1,0:T(1,128)}) custom-call(f32[32,8,1024]{2,1,0:T(8,128)} %sens.1, s32[8,32]{1,0:T(8,128)} %bitcast.7, s32[8,32]{1,0:T(8,128)} %bitcast.8, s32[1,32]{1,0:T(1,128)} %bitcast.9, s32[1,32]{1,0:T(1,128)} %bitcast.10, f32[1,32]{1,0:T(1,128)} %bitcast.11, s32[1,4,128]{2,1,0:T(4,128)} %hits_in.1), custom_call_target="tpu_custom_call" | custom-call | tf_op jit(solution)/shard_map/pallas_call | solution.py:447
  80.1 1.3 %shard_map.95 = (f32[1,4,128]{2,1,0:T(4,128)}, f32[8,128]{1,0:T(8,128)}, f32[1,32]{1,0:T(1,128)}) custom-call(f32[1,4,128]{2,1,0:T(4,128)} %get-tuple-element.9.model, f32[8,128]{1,0:T(8,128)} %get-tuple-element.10.station, f32[1,32]{1,0:T(1,128)} %get-tuple-element.11.ray), custom_call_target="tpu_custom_call" | custom-call | tf_op jit(solution)/shard_map/pallas_call | solution.py:483
